TPU v7x, 32 devices: a whole 2x2x4 slice. The times are simulated.
32 devices in a mesh: leaf: 8 (over y, x, core), col: 4 (over z).
Axes of the slice: x: 2, y: 2, z: 4, core: 2. Of those that a mesh axis runs over, the one named last changes fastest.
Arguments:
- histograms: bfloat16 [4, 32, 1024, 512], P(None, 'leaf', 'col'), may hold values from -6 to 6
- diag_inv: bfloat16 [4, 32, 512, 512], P(None, 'leaf', 'col'), as said below
- below_panel: bfloat16 [4, 32, 256, 512], P(None, 'leaf', 'col'), may hold values from -0.1875 to 0.1875
- parent_map: int32 [3, 32], P(None, 'leaf'), may hold values from 0 to 31, as said below
- row_lists: int32 [3, 32, 256], P(None, 'leaf'), may hold values from 0 to 511, as said below
Outputs:
- solution: bfloat16 [4, 32, 1024, 512], P(None, 'leaf', 'col')
- upward: bfloat16 [32, 1024, 256], P('leaf', 'col')
Inputs may be any that keep to these rules, and one draw needn't show every extreme that they name: `parent_map`: entry [l, j] names a supernode of tier l + 1 whose owner (index // 4) is the owner of supernode j (j // 4) or the leaf index that differs from it in bit l mod log2(8); at every tier some leaf index sends all its updates to that other index. `row_lists`: the 256 entries of each list are distinct. `diag_inv`: every block is lower triangular with a positive diagonal.
All inputs are finite; a program needn't handle non-finite values.
Results may differ from a plain program's by a relative error of at most 0.012.
Values may be sent and summed in bfloat16 or wider, within the bound.
No kernel may reach another device: no remote copies, remote signals or barrier semaphores. Data moves between devices by JAX's collectives and lax.ppermute only.
A program may use at most 64 MiB of HBM per device.

v0:
```python
import jax
import jax.numpy as jnp
from jax import lax
from jax.sharding import PartitionSpec as P


def swapped(block, axis, apart):
    count = lax.axis_size(axis)
    route = []
    for low in range(count):
        high = low | 1 << apart
        if high != low and high < count:
            route += [(low, high), (high, low)]
    return lax.ppermute(block, axis, route)


def spread_rows(update, lists, slots, per_device, node_width):
    slot_match = (
        slots[:, None, None, None] == jnp.arange(per_device, dtype=jnp.int32)[None, None, :, None]
    )
    row_match = (
        lists[:, :, None, None] == jnp.arange(node_width, dtype=jnp.int32)[None, None, None, :]
    )
    placing = jnp.logical_and(slot_match, row_match).astype(jnp.bfloat16)
    upper_part = update.astype(jnp.bfloat16)
    lower_part = (update - upper_part.astype(jnp.float32)).astype(jnp.bfloat16)
    first = jnp.einsum("scr,srpw->pcw", upper_part, placing, preferred_element_type=jnp.float32)
    second = jnp.einsum("scr,srpw->pcw", lower_part, placing, preferred_element_type=jnp.float32)
    return first + second


def route(update, targets, lists, bit_number, myself, per_device, node_width):
    owners = targets // per_device
    slots = targets % per_device
    staying = owners == myself
    self_slots = jnp.where(staying, slots, -1)
    peer_slots = jnp.where(staying, -1, slots)
    kept = spread_rows(update, lists, self_slots, per_device, node_width)
    leaving = spread_rows(update, lists, peer_slots, per_device, node_width)
    arrived = swapped(leaving.astype(jnp.bfloat16), "leaf", bit_number).astype(leaving.dtype)
    return kept + arrived


def on_device(histograms, diag_inv, below_panel, parent_map, row_lists):
    tier_count = histograms.shape[0]
    per_device = histograms.shape[1]
    node_width = histograms.shape[3]
    bit_count = max(lax.axis_size("leaf").bit_length() - 1, 1)
    myself = lax.axis_index("leaf")
    incoming = jnp.zeros(histograms.shape[1:], jnp.float32)
    solved = []
    upward = None
    for height in range(tier_count):
        source = (histograms[height].astype(jnp.float32) - incoming).astype(jnp.bfloat16)
        result = jnp.einsum(
            "scw,svw->scv",
            source,
            lax.all_gather(diag_inv[height], "col", axis=1, tiled=True),
            preferred_element_type=jnp.float32,
        )
        answer = result.astype(jnp.bfloat16)
        solved.append(answer)
        update = jnp.einsum(
            "scw,srw->scr",
            answer,
            lax.all_gather(below_panel[height], "col", axis=1, tiled=True),
            preferred_element_type=jnp.float32,
        )
        if height == tier_count - 1:
            upward = update.astype(jnp.bfloat16)
        else:
            incoming = route(
                update,
                parent_map[height],
                row_lists[height],
                height % bit_count,
                myself,
                per_device,
                node_width,
            )
    return (jnp.stack(solved), upward)


def solution(mesh):
    return jax.shard_map(
        on_device,
        mesh=mesh,
        in_specs=(
            P(None, "leaf", "col", None),
            P(None, "leaf", "col", None),
            P(None, "leaf", "col", None),
            P(None, "leaf"),
            P(None, "leaf", None),
        ),
        out_specs=(P(None, "leaf", "col", None), P("leaf", "col", None)),
        check_vma=False,
    )
```

profile of v0, /device:TPU:0, one launch (start us, length us, event | category | flops | bytes accessed | tf_op | source)
XLA Modules:
  0.0 322.3 jit_solution(12917312711124733408)
XLA Ops:
  7.2 2.9 fusion.68
  15.1 4.4 %broadcast_and_fusion.4 = (pred[4,256,4,512]{3,2,1,0:T(4,128)(4,1)S(1)}, pred[4,256,4,512]{3,2,1,0:T(4,128)(4,1)S(1)}) fusion(pred[4,4]{1,0:T(4,128)(4,1)S(1)} %get-tuple-element.40, pred[4,256,512]{2,1,0:T(8,128)(4,1)S(1)} %iota_compare_fusion.2, pred[4,4]{1,0:T(4,128)(4,1)S(1)} %get-tuple-element.41), kind=kLoop, calls=%fused_computation.5 | loop fusion | flops 4194304 | bytes 4718624 | tf_op jit(solution)/shard_map/and | solution.py:24
  19.5 5.4 %copy.10 = pred[4,256,4,512]{1,3,0,2:T(32,128)(4,1)} copy(pred[4,256,4,512]{3,2,1,0:T(4,128)(4,1)S(1)} %get-tuple-element.23) | data formatting | bytes 4194304 | tf_op jit(solution)/shard_map/and | solution.py:24
  26.6 32.3 %all-gather.17.cloned.1.call-done = bf16[1,4,512,512]{3,2,1,0:T(8,128)(2,1)} async-done(((bf16[1,4,128,512]{3,2,1,0:T(8,128)(2,1)}), bf16[1,4,512,512]{3,2,1,0:T(8,128)(2,1)}) %all-gather.17.cloned.1.call-update) | async-done | bytes 2097168 | tf_op jit(solution)/shard_map/all_gather | solution.py:58
  59.0 2.7 fusion.14
  61.6 25.6 %all-gather.19.cloned.1.call-done = bf16[1,4,256,512]{3,2,1,0:T(8,128)(2,1)} async-done(((bf16[1,4,64,512]{3,2,1,0:T(8,128)(2,1)}), bf16[1,4,256,512]{3,2,1,0:T(8,128)(2,1)}) %all-gather.19.cloned.1.call-update) | async-done | bytes 1048592 | tf_op jit(solution)/shard_map/all_gather | solution.py:66
  90.4 2.3 fusion.26
  92.8 5.1 %broadcast_and_fusion.2 = (pred[4,256,4,512]{3,2,1,0:T(4,128)(4,1)S(1)}, pred[4,256,4,512]{3,2,1,0:T(4,128)(4,1)}) fusion(pred[4,4]{1,0:T(4,128)(4,1)S(1)} %get-tuple-element.37, pred[4,256,512]{2,1,0:T(8,128)(4,1)S(1)} %copy-done.5, pred[4,4]{1,0:T(4,128)(4,1)S(1)} %iota_compare_fusion.6), kind=kLoop, calls=%fused_computation.3 | loop fusion | flops 4194304 | bytes 4718624 | tf_op jit(solution)/shard_map/and | solution.py:24
  97.9 5.5 %copy.7 = pred[4,256,4,512]{1,3,0,2:T(32,128)(4,1)S(1)} copy(pred[4,256,4,512]{3,2,1,0:T(4,128)(4,1)S(1)} %get-tuple-element.24) | data formatting | bytes 4194304 | tf_op jit(solution)/shard_map/and | solution.py:24
  103.4 5.5 %copy.16 = pred[4,256,4,512]{1,3,0,2:T(32,128)(4,1)} copy(pred[4,256,4,512]{3,2,1,0:T(4,128)(4,1)S(1)} %get-tuple-element.21) | data formatting | bytes 4194304 | tf_op jit(solution)/shard_map/and | solution.py:24
  109.0 2.7 fusion.51
  111.7 22.5 %all-gather.21.cloned.1.call-done = bf16[1,4,512,512]{3,2,1,0:T(8,128)(2,1)} async-done(((bf16[1,4,128,512]{3,2,1,0:T(8,128)(2,1)}), bf16[1,4,512,512]{3,2,1,0:T(8,128)(2,1)}) %all-gather.21.cloned.1.call-update) | async-done | bytes 2097168 | tf_op jit(solution)/shard_map/all_gather | solution.py:58
  134.2 6.1 %fusion.17 = bf16[4,256,512]{2,1,0:T(8,128)(2,1)S(1)} fusion(bf16[1,4,512,512]{3,2,1,0:T(8,128)(2,1)} %all-gather.21.cloned.1.call-done, f32[4,512,256,1]{1,2,3,0:T(8,128)} %fusion.51, bf16[4,256,512]{2,1,0:T(8,128)(2,1)} %collective-permute-done, pred[4,256,4,512]{1,3,0,2:T(32,128)(4,1)} %copy-done.9, bf16[4,4,256,512]{3,2,1,0:T(8,128)(2,1)} %param.5, ...), kind=kOutput, calls=%fused_computation.37 | convolution fusion | flops 1615331328 | bytes 10485760 | tf_op jit(solution)/shard_map/scw,svw->scv/dot_general | solution.py:55
  140.4 22.0 %all-gather.23.cloned.1.call-done = bf16[1,4,256,512]{3,2,1,0:T(8,128)(2,1)} async-done(((bf16[1,4,64,512]{3,2,1,0:T(8,128)(2,1)}), bf16[1,4,256,512]{3,2,1,0:T(8,128)(2,1)}) %all-gather.23.cloned.1.call-update) | async-done | bytes 1048592 | tf_op jit(solution)/shard_map/all_gather | solution.py:66
  162.4 1.8 fusion.32
  165.6 2.3 fusion.27
  169.4 4.3 %broadcast_and_fusion = (pred[4,256,4,512]{3,2,1,0:T(4,128)(4,1)S(1)}, pred[4,256,4,512]{3,2,1,0:T(4,128)(4,1)S(1)}) fusion(pred[4,4]{1,0:T(4,128)(4,1)S(1)} %get-tuple-element.36, pred[4,256,512]{2,1,0:T(8,128)(4,1)S(1)} %copy-done.4, pred[4,4]{1,0:T(4,128)(4,1)S(1)} %iota_compare_fusion.4), kind=kLoop, calls=%fused_computation.1 | loop fusion | flops 4194304 | bytes 4718624 | tf_op jit(solution)/shard_map/and | solution.py:24
  173.7 5.5 %copy.13 = pred[4,256,4,512]{1,3,0,2:T(32,128)(4,1)S(1)} copy(pred[4,256,4,512]{3,2,1,0:T(4,128)(4,1)S(1)} %copy-done) | data formatting | bytes 4194304 | tf_op jit(solution)/shard_map/and | solution.py:24
  179.3 5.4 %copy.22 = pred[4,256,4,512]{1,3,0,2:T(32,128)(4,1)} copy(pred[4,256,4,512]{3,2,1,0:T(4,128)(4,1)S(1)} %get-tuple-element.19) | data formatting | bytes 4194304 | tf_op jit(solution)/shard_map/and | solution.py:24
  184.7 2.6 fusion.47
  187.4 21.7 %all-gather.25.cloned.1.call-done = bf16[1,4,512,512]{3,2,1,0:T(8,128)(2,1)} async-done(((bf16[1,4,128,512]{3,2,1,0:T(8,128)(2,1)}), bf16[1,4,512,512]{3,2,1,0:T(8,128)(2,1)}) %all-gather.25.cloned.1.call-update) | async-done | bytes 2097168 | tf_op jit(solution)/shard_map/all_gather | solution.py:58
  209.1 7.1 %fusion.20 = bf16[4,256,512]{2,1,0:T(8,128)(2,1)} fusion(bf16[1,4,512,512]{3,2,1,0:T(8,128)(2,1)} %all-gather.25.cloned.1.call-done, f32[4,512,256,1]{1,2,3,0:T(8,128)} %fusion.47, bf16[4,256,512]{2,1,0:T(8,128)(2,1)} %collective-permute-done.1, pred[4,256,4,512]{1,3,0,2:T(32,128)(4,1)} %copy-done.10, bf16[4,4,256,512]{3,2,1,0:T(8,128)(2,1)} %param.5, ...), kind=kOutput, calls=%fused_computation.38 | convolution fusion | flops 1615331328 | bytes 10485760 | tf_op jit(solution)/shard_map/scw,svw->scv/dot_general | solution.py:55
  216.2 21.2 %all-gather.27.cloned.1.call-done = bf16[1,4,256,512]{3,2,1,0:T(8,128)(2,1)} async-done(((bf16[1,4,64,512]{3,2,1,0:T(8,128)(2,1)}), bf16[1,4,256,512]{3,2,1,0:T(8,128)(2,1)}) %all-gather.27.cloned.1.call-update) | async-done | bytes 1048592 | tf_op jit(solution)/shard_map/all_gather | solution.py:66
  237.4 2.2 fusion.30
  240.9 2.3 fusion.28
  244.7 5.5 %copy.19 = pred[4,256,4,512]{1,3,0,2:T(32,128)(4,1)S(1)} copy(pred[4,256,4,512]{3,2,1,0:T(4,128)(4,1)S(1)} %get-tuple-element.20) | data formatting | bytes 4194304 | tf_op jit(solution)/shard_map/and | solution.py:24
  251.6 2.6 fusion.43
  254.2 30.2 %all-gather.29.cloned.1.call-done = bf16[1,4,512,512]{3,2,1,0:T(8,128)(2,1)} async-done(((bf16[1,4,128,512]{3,2,1,0:T(8,128)(2,1)}), bf16[1,4,512,512]{3,2,1,0:T(8,128)(2,1)}) %all-gather.29.cloned.1.call-update) | async-done | bytes 2097168 | tf_op jit(solution)/shard_map/all_gather | solution.py:58
  284.4 7.1 %fusion.23 = bf16[4,256,512]{2,1,0:T(8,128)(2,1)} fusion(bf16[1,4,512,512]{3,2,1,0:T(8,128)(2,1)} %all-gather.29.cloned.1.call-done, f32[4,512,256,1]{1,2,3,0:T(8,128)} %fusion.43, bf16[4,256,512]{2,1,0:T(8,128)(2,1)} %collective-permute-done.2, pred[4,256,4,512]{1,3,0,2:T(32,128)(4,1)} %copy-done.11, bf16[4,4,256,512]{3,2,1,0:T(8,128)(2,1)} %param.5, ...), kind=kOutput, calls=%fused_computation.39 | convolution fusion | flops 1615331328 | bytes 10485760 | tf_op jit(solution)/shard_map/scw,svw->scv/dot_general | solution.py:55
  291.5 3.3 %pad_maximum_fusion = bf16[4,4,256,512]{3,2,1,0:T(8,128)(2,1)} fusion(bf16[1,4,256,512]{3,2,1,0:T(8,128)(2,1)} %bitcast.244, bf16[1,4,256,512]{3,2,1,0:T(8,128)(2,1)S(1)} %bitcast.243, bf16[1,4,256,512]{3,2,1,0:T(8,128)(2,1)S(1)} %bitcast.242, bf16[1,4,256,512]{3,2,1,0:T(8,128)(2,1)S(1)} %bitcast.241), kind=kLoop, calls=%fused_computation | loop fusion | flops 6291456 | bytes 8388608 | tf_op jit(solution)/shard_map/stack | solution.py:81
  294.9 17.8 %all-gather.31.cloned.1.call-done = bf16[1,4,256,512]{3,2,1,0:T(8,128)(2,1)} async-done(((bf16[1,4,64,512]{3,2,1,0:T(8,128)(2,1)}), bf16[1,4,256,512]{3,2,1,0:T(8,128)(2,1)}) %all-gather.31.cloned.1.call-update) | async-done | bytes 1048592 | tf_op jit(solution)/shard_map/all_gather | solution.py:66
  312.7 2.8 convolution_convert_fusion
  (75 shorter events, 16.9 us)
Async XLA Ops:
  7.2 3.1 copy-start.16
  7.2 51.8 %all-gather.17.cloned.1.call-start = ((), (), s32[]{:S(2)}) async-start(), calls=%async_computation | async-start | bytes 2621440 | tf_op jit(solution)/shard_map/all_gather | solution.py:58
  10.2 4.4 %copy-start.17 = (s32[3,4,256]{2,1,0:T(4,128)S(1)}, s32[3,4,256]{2,1,0:T(4,128)}, u32[]{:S(2)}) copy-start(s32[3,4,256]{2,1,0:T(4,128)} %param.9) | copy-start | bytes 36868
  10.2 4.8 %copy-start.18 = (s32[3,4]{1,0:T(4,128)S(1)}, s32[3,4]{1,0:T(4,128)}, u32[]{:S(2)}) copy-start(s32[3,4]{1,0:T(4,128)} %param.8) | copy-start | bytes 148
  10.2 77.0 %all-gather.19.cloned.1.call-start = ((), (), s32[]{:S(2)}) async-start(), calls=%async_computation.1 | async-start | bytes 1310720 | tf_op jit(solution)/shard_map/all_gather | solution.py:66
  11.3 122.9 %all-gather.21.cloned.1.call-start = ((), (), s32[]{:S(2)}) async-start(), calls=%async_computation.2 | async-start | bytes 2621440 | tf_op jit(solution)/shard_map/all_gather | solution.py:58
  12.0 150.3 %all-gather.23.cloned.1.call-start = ((), (), s32[]{:S(2)}) async-start(), calls=%async_computation.3 | async-start | bytes 1310720 | tf_op jit(solution)/shard_map/all_gather | solution.py:66
  12.6 196.5 %all-gather.25.cloned.1.call-start = ((), (), s32[]{:S(2)}) async-start(), calls=%async_computation.4 | async-start | bytes 2621440 | tf_op jit(solution)/shard_map/all_gather | solution.py:58
  13.2 224.2 %all-gather.27.cloned.1.call-start = ((), (), s32[]{:S(2)}) async-start(), calls=%async_computation.5 | async-start | bytes 1310720 | tf_op jit(solution)/shard_map/all_gather | solution.py:66
  13.8 270.6 %all-gather.29.cloned.1.call-start = ((), (), s32[]{:S(2)}) async-start(), calls=%async_computation.6 | async-start | bytes 2621440 | tf_op jit(solution)/shard_map/all_gather | solution.py:58
  14.5 298.1 %all-gather.31.cloned.1.call-start = ((), (), s32[]{:S(2)}) async-start(), calls=%async_computation.7 | async-start | bytes 1310720 | tf_op jit(solution)/shard_map/all_gather | solution.py:66
  87.2 1.9 copy-start.6
  89.1 19.8 %copy-start.12 = (f32[4,256,256]{2,1,0:T(8,128)}, f32[4,256,256]{2,1,0:T(8,128)S(1)}, u32[]{:S(2)}) copy-start(f32[4,256,256]{2,1,0:T(8,128)S(1)} %fusion.34) | copy-start | bytes 3145732
  90.4 2.3 copy-start.5
  92.8 41.5 %collective-permute-start = (bf16[4,256,512]{2,1,0:T(8,128)(2,1)}, bf16[4,256,512]{2,1,0:T(8,128)(2,1)}, u32[]{:S(2)}, u32[]{:S(2)}) collective-permute-start(bf16[4,256,512]{2,1,0:T(8,128)(2,1)} %fusion.26), channel_id=1, source_target_pairs={{0,4},{4,0},{8,12},{12,8},{16,20},{20,16},{24,28},{28,24},{1,5},{5... | collective-permute-start | bytes 3145736 | tf_op jit(solution)/shard_map/ppermute | solution.py:14
  103.4 5.6 %copy-start.9 = (pred[4,256,4,512]{1,3,0,2:T(32,128)(4,1)}, pred[4,256,4,512]{1,3,0,2:T(32,128)(4,1)S(1)}, u32[]{:S(2)}) copy-start(pred[4,256,4,512]{1,3,0,2:T(32,128)(4,1)S(1)} %copy.7) | copy-start | bytes 6291460
  140.4 25.2 %copy-start.1 = (bf16[4,256,512]{2,1,0:T(8,128)(2,1)}, bf16[4,256,512]{2,1,0:T(8,128)(2,1)S(1)}, u32[]{:S(2)}) copy-start(bf16[4,256,512]{2,1,0:T(8,128)(2,1)S(1)} %fusion.17) | copy-start | bytes 3145732
  162.4 1.9 copy-start.7
  164.3 20.4 %copy-start.13 = (f32[4,256,256]{2,1,0:T(8,128)}, f32[4,256,256]{2,1,0:T(8,128)S(1)}, u32[]{:S(2)}) copy-start(f32[4,256,256]{2,1,0:T(8,128)S(1)} %fusion.32) | copy-start | bytes 3145732
  165.6 3.8 %copy-start.4 = (pred[4,256,512]{2,1,0:T(8,128)(4,1)S(1)}, pred[4,256,512]{2,1,0:T(8,128)(4,1)}, u32[]{:S(2)}) copy-start(pred[4,256,512]{2,1,0:T(8,128)(4,1)} %get-tuple-element.38) | copy-start | bytes 1572868
  167.9 41.2 %collective-permute-start.1 = (bf16[4,256,512]{2,1,0:T(8,128)(2,1)}, bf16[4,256,512]{2,1,0:T(8,128)(2,1)}, u32[]{:S(2)}, u32[]{:S(2)}) collective-permute-start(bf16[4,256,512]{2,1,0:T(8,128)(2,1)} %fusion.27), channel_id=1, source_target_pairs={{0,8},{8,0},{4,12},{12,4},{16,24},{24,16},{20,28},{28,20},{1,9},{9... | collective-permute-start | bytes 3145736 | tf_op jit(solution)/shard_map/ppermute | solution.py:14
  169.4 4.4 %copy-start = (pred[4,256,4,512]{3,2,1,0:T(4,128)(4,1)S(1)}, pred[4,256,4,512]{3,2,1,0:T(4,128)(4,1)}, u32[]{:S(2)}) copy-start(pred[4,256,4,512]{3,2,1,0:T(4,128)(4,1)} %get-tuple-element.22) | copy-start | bytes 6291460
  179.3 5.5 %copy-start.10 = (pred[4,256,4,512]{1,3,0,2:T(32,128)(4,1)}, pred[4,256,4,512]{1,3,0,2:T(32,128)(4,1)S(1)}, u32[]{:S(2)}) copy-start(pred[4,256,4,512]{1,3,0,2:T(32,128)(4,1)S(1)} %copy.13) | copy-start | bytes 6291460
  237.4 2.2 copy-start.8
  239.6 1.3 copy-start.14
  243.2 41.2 %collective-permute-start.2 = (bf16[4,256,512]{2,1,0:T(8,128)(2,1)}, bf16[4,256,512]{2,1,0:T(8,128)(2,1)}, u32[]{:S(2)}, u32[]{:S(2)}) collective-permute-start(bf16[4,256,512]{2,1,0:T(8,128)(2,1)} %fusion.28), channel_id=1, source_target_pairs={{0,16},{16,0},{4,20},{20,4},{8,24},{24,8},{12,28},{28,12},{1,17},{... | collective-permute-start | bytes 3145736 | tf_op jit(solution)/shard_map/ppermute | solution.py:14
  244.7 6.9 %copy-start.15 = (f32[4,256,256]{2,1,0:T(8,128)S(1)}, f32[4,256,256]{2,1,0:T(8,128)}, u32[]{:S(2)}) copy-start(f32[4,256,256]{2,1,0:T(8,128)} %copy-done.14) | copy-start | bytes 3145732
  250.2 1.4 copy-start.11
  254.2 37.3 %copy-start.2 = (bf16[4,256,512]{2,1,0:T(8,128)(2,1)S(1)}, bf16[4,256,512]{2,1,0:T(8,128)(2,1)}, u32[]{:S(2)}) copy-start(bf16[4,256,512]{2,1,0:T(8,128)(2,1)} %copy-done.1) | copy-start | bytes 3145732
  254.2 37.3 %copy-start.3 = (bf16[4,256,512]{2,1,0:T(8,128)(2,1)S(1)}, bf16[4,256,512]{2,1,0:T(8,128)(2,1)}, u32[]{:S(2)}) copy-start(bf16[4,256,512]{2,1,0:T(8,128)(2,1)} %fusion.20) | copy-start | bytes 3145732
Sparse Core Ops, SparseCore 0:
  10.3 48.6 all-gather.16
  60.5 26.6 all-gather.18
  88.8 45.3 all-gather.20
  135.6 26.6 all-gather.22
  163.8 45.2 all-gather.24
  210.5 26.8 all-gather.26
  238.9 45.4 all-gather.28
  286.0 26.6 all-gather.30
where the time goes:
time: 323 us; the launch traced here: 322 us
  waiting for transfers between devices  196 us (61%)
  matrix products  50.4 us (16%)
  local copies, waits for them, and re-layouts  38.4 us (12%)
  other arithmetic  19.5 us (6%)
  between operations  14.4 us (4%)
  starting transfers between devices  3.26 us (1%)
    all_gather x4, waiting for transfers between devices, on_device(): lax.all_gather(diag_inv[height], 'col', axis=1, tiled=True)  107 us
    all_gather x4, waiting for transfers between devices, on_device(): lax.all_gather(below_panel[height], 'col', axis=1, tiled=True)  86.5 us
    and x6, local copies, waits for them, and re-layouts, spread_rows(): placing = jnp.logical_and(slot_match, row_match).astype(jnp.bfloat16)  32.9 us
    dot_general x4, matrix products, on_device(): jnp.einsum('scw,svw->scv', source, lax.all_gather(diag_inv[height], 'col'...  23 us
    and x3, other arithmetic, spread_rows(): placing = jnp.logical_and(slot_match, row_match).astype(jnp.bfloat16)  13.8 us
    dot_general x6, matrix products, spread_rows(): jnp.einsum('scr,srpw->pcw', upper_part, placing, preferred_element_type=j...  11.9 us
    dot_general x4, matrix products, on_device(): jnp.einsum('scw,srw->scr', answer, lax.all_gather(below_panel[height], 'c...  8.62 us
    dot_general x3, matrix products, spread_rows(): jnp.einsum('scr,srpw->pcw', lower_part, placing, preferred_element_type=j...  6.89 us
  transfers between devices with their start and end apart: 11, of which 8 were waited for; matrix products, arithmetic and copies ran while one was open for 31% of the time, Pallas kernels for 0%

commit v1 on v0

v1 whole, which is shorter than its diff:
```python
import functools

import jax
import jax.numpy as jnp
from jax import lax
from jax.experimental import pallas as pl
from jax.experimental.pallas import tpu as pltpu
from jax.sharding import PartitionSpec as P

LANES = 128
SPARE = 16
ANY = pl.BlockSpec(memory_space=pl.ANY)
SMEM = pl.BlockSpec(memory_space=pltpu.SMEM)


def swap_route(axis, apart):
    count = lax.axis_size(axis)
    pairs = []
    for low in range(count):
        high = low | 1 << apart
        if high != low and high < count:
            pairs += [(low, high), (high, low)]
    return pairs


def dot_rows(left, right):
    return lax.dot_general(
        left, right, (((1,), (1,)), ((), ())), preferred_element_type=jnp.float32
    )


def spread_rows(update, lists, slots, per_device, node_width):
    slot_match = (
        slots[:, None, None, None] == jnp.arange(per_device, dtype=jnp.int32)[None, None, :, None]
    )
    row_match = (
        lists[:, :, None, None] == jnp.arange(node_width, dtype=jnp.int32)[None, None, None, :]
    )
    placing = jnp.logical_and(slot_match, row_match).astype(jnp.bfloat16)
    return jnp.einsum(
        "scr,srpw->pcw", update.astype(jnp.bfloat16), placing, preferred_element_type=jnp.float32
    )


def gathered_plan(histograms, diag_inv, below_panel, parent_map, row_lists):
    tier_count, per_device, _, node_width = histograms.shape
    bit_count = max(lax.axis_size("leaf").bit_length() - 1, 1)
    myself = lax.axis_index("leaf")
    incoming = jnp.zeros(histograms.shape[1:], jnp.float32)
    solved = []
    for height in range(tier_count):
        source = (histograms[height].astype(jnp.float32) - incoming).astype(jnp.bfloat16)
        diag = lax.all_gather(diag_inv[height], "col", axis=1, tiled=True)
        below = lax.all_gather(below_panel[height], "col", axis=1, tiled=True)
        answer = jnp.einsum(
            "scw,svw->scv", source, diag, preferred_element_type=jnp.float32
        ).astype(jnp.bfloat16)
        solved.append(answer)
        update = jnp.einsum("scw,srw->scr", answer, below, preferred_element_type=jnp.float32)
        if height == tier_count - 1:
            break
        owners = parent_map[height] // per_device
        slots = parent_map[height] % per_device
        staying = owners == myself
        lists = row_lists[height]
        kept = spread_rows(update, lists, jnp.where(staying, slots, -1), per_device, node_width)
        leaving = spread_rows(update, lists, jnp.where(staying, -1, slots), per_device, node_width)
        path = swap_route("leaf", height % bit_count)
        arrived = lax.ppermute(leaving.astype(jnp.bfloat16), "leaf", path)
        incoming = kept + arrived.astype(jnp.float32)
    return jnp.stack(solved), update.astype(jnp.bfloat16)


def layout(per_device, below_rows, node_width):
    block = per_device * LANES
    tri = block // 2
    below = per_device * below_rows * (node_width // LANES)
    return block, tri, below, block + tri + SPARE + below


def pack_kernel(place_ref, diag_ref, below_ref, base_ref, rest_ref):
    per_device, below_rows, node_width = below_ref.shape[1:]
    block, tri, _, total = layout(per_device, below_rows, node_width)
    for s in range(per_device):
        rows = slice(s * LANES, (s + 1) * LANES)
        base_ref[rows, :] = diag_ref[0, s, :, :LANES]
        for k in range(3):
            rest_ref[k * block + s * LANES : k * block + (s + 1) * LANES, :] = diag_ref[
                0, s, :, k * LANES : (k + 1) * LANES
            ]
        start = block + tri + SPARE + s * below_rows * (node_width // LANES)
        for k in range(node_width // LANES):
            base_ref[start + k * below_rows : start + (k + 1) * below_rows, :] = below_ref[
                0, s, :, k * LANES : (k + 1) * LANES
            ]
    rest_ref[3 * block :, :] = jnp.zeros((total - 3 * block, LANES), rest_ref.dtype)
    down = lax.broadcasted_iota(jnp.int32, (LANES, LANES), 0)
    across = lax.broadcasted_iota(jnp.int32, (LANES, LANES), 1)
    for place in range(4):

        @pl.when(place_ref[0] == place)
        def _():
            columns = slice(place * LANES, (place + 1) * LANES)
            pivots = []
            for pair in range(per_device // 2):
                first = diag_ref[0, 2 * pair, :, columns].astype(jnp.float32)
                second = diag_ref[0, 2 * pair + 1, :, columns].astype(jnp.float32)
                both = jnp.where(down >= across, first, second.T)
                base_ref[block + pair * LANES : block + (pair + 1) * LANES, :] = both.astype(
                    base_ref.dtype
                )
                pivots.append(
                    jnp.sum(jnp.where(down == across, second, 0.0), axis=0, keepdims=True)
                )
            pivots.append(jnp.zeros((SPARE - len(pivots), LANES), jnp.float32))
            base_ref[block + tri : block + tri + SPARE, :] = jnp.concatenate(pivots, 0).astype(
                base_ref.dtype
            )


def pack(place, diag_inv, below_panel, height):
    _, per_device, rows, node_width = diag_inv.shape
    below_rows = below_panel.shape[2]
    total = layout(per_device, below_rows, node_width)[-1]
    shape = jax.ShapeDtypeStruct((total, LANES), diag_inv.dtype)
    return pl.pallas_call(
        pack_kernel,
        grid=(1,),
        in_specs=[
            SMEM,
            pl.BlockSpec((1, per_device, rows, node_width), lambda i: (height, 0, 0, 0)),
            pl.BlockSpec((1, per_device, below_rows, node_width), lambda i: (height, 0, 0, 0)),
        ],
        out_specs=[pl.BlockSpec((total, LANES), lambda i: (0, 0))] * 2,
        out_shape=[shape, shape],
        cost_estimate=pl.CostEstimate(
            flops=0, bytes_accessed=4 * total * LANES * 2, transcendentals=0
        ),
        name=f"pack_{height}",
    )(place, diag_inv, below_panel)


def source_kernel(slots_ref, hist_ref, own_ref, peer_ref, own_lists, peer_lists, out_ref, total):
    per_device, below = own_ref.shape[0], own_ref.shape[2]
    width = out_ref.shape[2]
    total[...] = hist_ref[0].astype(jnp.float32)
    target = lax.broadcasted_iota(jnp.int32, (width, below), 0)
    for refs in ((own_ref, own_lists, 0), (peer_ref, peer_lists, per_device)):
        update_ref, lists_ref, offset = refs
        for s in range(per_device):
            slot = slots_ref[offset + s]

            @pl.when(slot >= 0)
            def _():
                here = target == lists_ref[s : s + 1, :]
                placing = jnp.where(here, 1.0, 0.0).astype(jnp.bfloat16)
                total[slot] = total[slot] - dot_rows(update_ref[s], placing)

    out_ref[...] = total[...].astype(out_ref.dtype)


def source_of(histograms, height, own, peer, slots, own_lists, peer_lists):
    _, per_device, columns, width = histograms.shape
    below = own.shape[2]
    whole = pl.BlockSpec((per_device, columns, below), lambda i: (0, 0, 0))
    lists = pl.BlockSpec((per_device, below), lambda i: (0, 0))
    return pl.pallas_call(
        source_kernel,
        grid=(1,),
        in_specs=[
            SMEM,
            pl.BlockSpec((1, per_device, columns, width), lambda i: (height, 0, 0, 0)),
            whole,
            whole,
            lists,
            lists,
        ],
        out_specs=pl.BlockSpec((per_device, columns, width), lambda i: (0, 0, 0)),
        out_shape=jax.ShapeDtypeStruct((per_device, columns, width), jnp.bfloat16),
        scratch_shapes=[pltpu.VMEM((per_device, columns, width), jnp.float32)],
        compiler_params=pltpu.CompilerParams(vmem_limit_bytes=32 << 20),
        cost_estimate=pl.CostEstimate(
            flops=4 * per_device * columns * width * below,
            bytes_accessed=6 * per_device * columns * width,
            transcendentals=0,
        ),
        name=f"source_{height}",
    )(slots, histograms, own, peer, own_lists, peer_lists)


def solve_kernel(
    group_at,
    has_prior,
    place_ref,
    source_ref,
    base,
    rest,
    left0,
    left1,
    left2,
    left3,
    right0,
    right1,
    right2,
    *refs,
):
    if has_prior:
        refs = refs[1:]
    solved_ref, update_ref, tail, off, diag, below, sems = refs
    below_width = below.shape[1]
    below_rows = below.shape[0] // 4
    block = off.shape[0] // 6
    tri = block // 2
    step = pl.program_id(0)

    @pl.when(step == 0)
    def _():
        def head(ref):
            return ref.at[pl.ds(0, block)]

        def foot(ref):
            return ref.at[pl.ds(block, tail.shape[1])]

        def all_off(ref):
            return ref.at[pl.ds(0, 3 * block)]

        r0, r1, r2 = (r.at[group_at] for r in (right0, right1, right2))
        second = rest.at[pl.ds(block, block)]
        where = (
            (foot(base), foot(left0), foot(left1), foot(left2),
             head(left0), head(left1), head(left2), all_off(left3)),
            (foot(r0), foot(base), foot(left0), foot(left1),
             head(base), head(left0), head(left1), all_off(left2)),
            (foot(r1), foot(r0), foot(base), foot(left0),
             head(r0), head(base), second, all_off(left1)),
            (foot(r2), foot(r1), foot(r0), foot(base),
             head(r1), head(r0), head(r2), all_off(rest)),
        )
        into = [tail.at[j] for j in range(4)]
        into += [off.at[pl.ds(k * block, block)] for k in range(3)]
        into += [off.at[pl.ds(3 * block, 3 * block)]]
        for place in range(4):

            @pl.when(place_ref[0] == place)
            def _():
                copies = [
                    pltpu.make_async_copy(src, dst, sems.at[i])
                    for i, (src, dst) in enumerate(zip(where[place], into))
                ]
                for copy in copies:
                    copy.start()
                for copy in copies:
                    copy.wait()

    down = lax.broadcasted_iota(jnp.int32, (LANES, LANES), 0)
    across = lax.broadcasted_iota(jnp.int32, (LANES, LANES), 1)
    zero = jnp.zeros((LANES, LANES), diag.dtype)
    per_step = solved_ref.shape[1]
    for part in range(per_step):
        s = step * per_step + part
        row = pl.multiple_of(s * LANES, LANES)
        spot = 0
        for j in range(4):
            rows = slice(j * LANES, (j + 1) * LANES)
            for k in range(j):
                diag[part, rows, k * LANES : (k + 1) * LANES] = off[
                    pl.ds(pl.multiple_of(spot * block + row, LANES), LANES), :
                ]
                spot += 1
            pair = pl.multiple_of(step * LANES, LANES)
            both = tail[j, pl.ds(pair, LANES), :].astype(jnp.float32)
            if part == 0:
                mine = jnp.where(down >= across, both, 0.0)
            else:
                pivots = tail[j, tri : tri + SPARE, :].astype(jnp.float32)
                which = lax.broadcasted_iota(jnp.int32, (SPARE, LANES), 0) == step
                pivot = jnp.sum(jnp.where(which, pivots, 0.0), axis=0, keepdims=True)
                mine = jnp.where(
                    down > across, both.T, jnp.where(down == across, pivot, 0.0)
                )
            diag[part, rows, rows] = mine.astype(diag.dtype)
            if j % 2 == 0:
                diag[part, rows, (j + 1) * LANES : (j + 2) * LANES] = zero
            first = tri + SPARE + s * below_rows * (below_width // LANES)
            for k in range(below_width // LANES):
                below[j * below_rows : (j + 1) * below_rows, k * LANES : (k + 1) * LANES] = tail[
                    j, pl.ds(pl.multiple_of(first + k * below_rows, 16), below_rows), :
                ]
        half = 2 * LANES
        x = source_ref[part]
        solved_ref[0, part, :, :half] = dot_rows(
            x[:, :half], diag[part, :half, :half]
        ).astype(solved_ref.dtype)
        solved_ref[0, part, :, half:] = dot_rows(x, diag[part, half:, :]).astype(solved_ref.dtype)
        update_ref[part] = dot_rows(solved_ref[0, part], below[...]).astype(update_ref.dtype)


def solve(place, source, first_block, height, sizes, own, lefts, rights, group_at, prior):
    tiers, per_device, below_rows = sizes
    _, columns, width = source.shape
    below = 4 * below_rows
    block, _, _, total = layout(per_device, below_rows, width)
    has_prior = prior is not None
    operands = [place, source, *own, *lefts, *rights] + ([prior] if has_prior else [])
    return pl.pallas_call(
        functools.partial(solve_kernel, group_at, has_prior),
        grid=(per_device // 2,),
        in_specs=[SMEM, pl.BlockSpec((2, columns, width), lambda i: (first_block + i, 0, 0))]
        + [ANY] * (len(operands) - 2),
        out_specs=[
            pl.BlockSpec((1, 2, columns, width), lambda i: (height, i, 0, 0)),
            pl.BlockSpec((2, columns, below), lambda i: (i, 0, 0)),
        ],
        out_shape=[
            jax.ShapeDtypeStruct((tiers, per_device, columns, width), jnp.bfloat16),
            jax.ShapeDtypeStruct((per_device, columns, below), jnp.bfloat16),
        ],
        scratch_shapes=[
            pltpu.VMEM((4, total - block, LANES), jnp.bfloat16),
            pltpu.VMEM((6 * block, LANES), jnp.bfloat16),
            pltpu.VMEM((2, width, width), jnp.bfloat16),
            pltpu.VMEM((below, width), jnp.bfloat16),
            pltpu.SemaphoreType.DMA((8,)),
        ],
        input_output_aliases={len(operands) - 1: 0} if has_prior else {},
        compiler_params=pltpu.CompilerParams(vmem_limit_bytes=32 << 20),
        cost_estimate=pl.CostEstimate(
            flops=2 * per_device * columns * width * (width + below),
            bytes_accessed=6 * per_device * columns * width,
            transcendentals=0,
        ),
        name=f"solve_{height}",
    )(*operands)


def after(value, *earlier):
    return lax.optimization_barrier((value, *(e.reshape(-1, LANES)[:8] for e in earlier)))[0]


def send(value, route):
    return lax.ppermute(value, "col", route)


def line_plan(histograms, diag_inv, below_panel, parent_map, row_lists):
    tiers, per_device, columns, width = histograms.shape
    below_rows = below_panel.shape[2]
    block, _, _, total = layout(per_device, below_rows, width)
    place = lax.axis_index("col").astype(jnp.int32)
    place_ref = place[None]
    up = [(0, 1), (1, 2), (2, 3)]
    down = [(1, 0), (2, 1), (3, 2)]
    packs = [pack(place_ref, diag_inv, below_panel, t) for t in range(tiers)]

    lefts = []
    for base, rest in packs:
        left0 = send(base, down)
        mixed = jnp.concatenate([rest[block : 2 * block], left0[block:]], 0)
        left1 = send(jnp.where(place == 1, left0, jnp.where(place == 2, mixed, rest)), down)
        left2 = send(left1, down[:2])
        left3 = send(left2[: 3 * block], down[:1])
        lefts.append((left0, left1, left2, left3))

    rights = []
    for group in right_groups(tiers):
        bases = jnp.stack([packs[t][0] for t in group])
        if group[0] > 0:
            bases = after(bases, lefts[0][1])
        right0 = send(bases, up)
        right1 = send(right0, up[1:])
        second = jnp.stack([packs[t][1][block : 2 * block] for t in group])
        right2 = send(jnp.concatenate([second, right1[:, block:]], 1), up[2:])
        rights += [((right0, right1, right2), i) for i in range(len(group))]

    myself = lax.axis_index("leaf")
    count = lax.axis_size("leaf")
    bit_count = max(count.bit_length() - 1, 1)
    table = jnp.concatenate([parent_map[:, :, None], row_lists], 2)
    tables = lax.all_gather(table, "leaf")
    source, first_block = histograms.reshape(-1, columns, width), 0
    solved = None
    for t in range(tiers):
        right, group_at = rights[t]
        solved, update = solve(
            place_ref,
            source,
            first_block,
            t,
            (tiers, per_device, below_rows),
            packs[t],
            lefts[t],
            right,
            group_at,
            solved,
        )
        if t == tiers - 1:
            break
        bit = t % bit_count
        peer = lax.ppermute(update, "leaf", swap_route("leaf", bit))
        partner = jnp.bitwise_xor(myself, 1 << bit)
        theirs = lax.dynamic_index_in_dim(tables, jnp.minimum(partner, count - 1), 0, False)[t]
        parents = jnp.concatenate([parent_map[t], theirs[:, 0]])
        exists = jnp.repeat(jnp.stack([partner >= 0, partner < count]), per_device)
        mine = jnp.logical_and(parents // per_device == myself, exists)
        slots = jnp.where(mine, parents % per_device, -1)
        source = source_of(histograms, t + 1, update, peer, slots, row_lists[t], theirs[:, 1:])
        first_block = 0
    return solved, update


def right_groups(tiers):
    return [[0], list(range(1, tiers))]


def on_device(histograms, diag_inv, below_panel, parent_map, row_lists):
    _, per_device, rows, width = diag_inv.shape
    fits = (
        lax.axis_size("col") == 4
        and rows == LANES
        and width == 4 * rows
        and per_device % 2 == 0
        and per_device <= 2 * SPARE
        and below_panel.shape[2] % 16 == 0
        and histograms.shape[2] % 16 == 0
        and histograms.shape[0] > 1
    )
    plan = line_plan if fits else gathered_plan
    return plan(histograms, diag_inv, below_panel, parent_map, row_lists)


def solution(mesh):
    return jax.shard_map(
        on_device,
        mesh=mesh,
        in_specs=(
            P(None, "leaf", "col", None),
            P(None, "leaf", "col", None),
            P(None, "leaf", "col", None),
            P(None, "leaf"),
            P(None, "leaf", None),
        ),
        out_specs=(P(None, "leaf", "col", None), P("leaf", "col", None)),
        check_vma=False,
    )
```

time: 323 us -> 208 us (0.64)
  waiting for transfers between devices: 196 us -> 95.3 us
  matrix products: 50.4 us -> 0 us
  starting transfers between devices: 3.26 us -> 37.1 us
  Pallas kernels: 0 us -> 32.3 us
  local copies, waits for them, and re-layouts: 38.4 us -> 21.7 us
  between operations: 14.4 us -> 1.43 us
  other arithmetic: 19.5 us -> 7.57 us
  blocking collectives: 0 us -> 9.25 us
    all_gather x8 -> x0, waiting for transfers between devices: 193 us -> none  [the longest x4 107 us: on_device(): lax.all_gather(diag_inv[height], 'col', axis=1, tiled=True)]
    ppermute x3 -> x25, waiting for transfers between devices: 0.01 us -> 95.3 us  [the longest x22 88.6 us: send(): return lax.ppermute(value, 'col', route)]
    dot_general x17 -> x0, matrix products: 50.4 us -> none  [the longest x4 23 us: on_device(): jnp.einsum('scw,svw->scv', source, lax.all_gather(diag_inv[height], 'col'...]
    ppermute x3 -> x25, starting transfers between devices: 2.95 us -> 37.1 us  [the longest x22 33.9 us: send(): return lax.ppermute(value, 'col', route)]
    and x6 -> x0, local copies, waits for them, and re-layouts: 32.9 us -> none  [spread_rows(): placing = jnp.logical_and(slot_match, row_match).astype(jnp.bfloat16)]
    pallas_call x0 -> x11, Pallas kernels: none -> 32.3 us  [the longest x4 15.8 us: solve(): pl.pallas_call(functools.partial(solve_kernel, group_at, has_prior), grid...]
    and x3 -> x0, other arithmetic: 13.8 us -> none  [spread_rows(): placing = jnp.logical_and(slot_match, row_match).astype(jnp.bfloat16)]
    all_gather x0 -> x1, blocking collectives: none -> 9.25 us  [line_plan(): tables = lax.all_gather(table, 'leaf')]
  transfers between devices with their start and end apart: 11 -> 25, of which waited for: 8 -> 12; matrix products, arithmetic and copies ran while one was open for 31% -> 9% of each run, Pallas kernels for 0% -> 10%
where the time goes in v1:
time: 208 us; the launch traced here: 205 us
  waiting for transfers between devices  95.3 us (46%)
  starting transfers between devices  37.1 us (18%)
  Pallas kernels  32.3 us (16%)
  local copies, waits for them, and re-layouts  21.7 us (10%)
  blocking collectives  9.25 us (4%)
  other arithmetic  7.57 us (4%)
    ppermute x22, waiting for transfers between devices, send(): return lax.ppermute(value, 'col', route)  88.6 us
    ppermute x22, starting transfers between devices, send(): return lax.ppermute(value, 'col', route)  33.9 us
    pallas_call x4, Pallas kernels, solve(): pl.pallas_call(functools.partial(solve_kernel, group_at, has_prior), grid...  15.8 us
    pallas_call x4, Pallas kernels, pack(): pl.pallas_call(pack_kernel, grid=(1,), in_specs=[SMEM, pl.BlockSpec((1, p...  9.27 us
    all_gather x1, blocking collectives, line_plan(): tables = lax.all_gather(table, 'leaf')  9.25 us
    unnamed x54, local copies, waits for them, and re-layouts  8.48 us
    pallas_call x3, Pallas kernels, source_of(): pl.pallas_call(source_kernel, grid=(1,), in_specs=[SMEM, pl.BlockSpec((1,...  7.25 us
    ppermute x3, waiting for transfers between devices, line_plan(): peer = lax.ppermute(update, 'leaf', swap_route('leaf', bit))  6.76 us
  transfers between devices with their start and end apart: 25, of which 12 were waited for; matrix products, arithmetic and copies ran while one was open for 9% of the time, Pallas kernels for 10%

profile of v1, /device:TPU:0, one launch (start us, length us, event | category | flops | bytes accessed | tf_op | source)
XLA Modules:
  0.0 204.7 jit_solution(11975200253850353834)
XLA Ops:
  0.6 2.3 %pack_1.1 = (bf16[1808,128]{1,0:T(8,128)(2,1)}, bf16[1808,128]{1,0:T(8,128)(2,1)}) custom-call(s32[1]{0:T(128)} %bitcast.place_ref, bf16[4,4,128,512]{3,2,1,0:T(8,128)(2,1)} %diag_ref.7, bf16[4,4,64,512]{3,2,1,0:T(8,128)(2,1)} %below_ref.7), custom_call_target="tpu_custom_call" | custom-call | bytes 1851392 | tf_op jit(solution)/shard_map/pack_1/pallas_call | solution.py:126
  3.0 2.3 %pack_3.1 = (bf16[1808,128]{1,0:T(8,128)(2,1)}, bf16[1808,128]{1,0:T(8,128)(2,1)}) custom-call(s32[1]{0:T(128)} %bitcast.place_ref, bf16[4,4,128,512]{3,2,1,0:T(8,128)(2,1)} %diag_ref.7, bf16[4,4,64,512]{3,2,1,0:T(8,128)(2,1)} %below_ref.7), custom_call_target="tpu_custom_call" | custom-call | bytes 1851392 | tf_op jit(solution)/shard_map/pack_3/pallas_call | solution.py:126
  5.2 2.3 %pack_2.1 = (bf16[1808,128]{1,0:T(8,128)(2,1)}, bf16[1808,128]{1,0:T(8,128)(2,1)}) custom-call(s32[1]{0:T(128)} %bitcast.place_ref, bf16[4,4,128,512]{3,2,1,0:T(8,128)(2,1)} %diag_ref.7, bf16[4,4,64,512]{3,2,1,0:T(8,128)(2,1)} %below_ref.7), custom_call_target="tpu_custom_call" | custom-call | bytes 1851392 | tf_op jit(solution)/shard_map/pack_2/pallas_call | solution.py:126
  7.5 2.5 %pad_maximum_fusion = bf16[3,1808,128]{2,1,0:T(8,128)(2,1)} fusion(bf16[1,1808,128]{2,1,0:T(8,128)(2,1)} %bitcast.21, bf16[1,1808,128]{2,1,0:T(8,128)(2,1)} %bitcast.20, bf16[1,1808,128]{2,1,0:T(8,128)(2,1)} %bitcast.19), kind=kLoop, calls=%fused_computation | loop fusion | flops 1388544 | bytes 2777088 | tf_op jit(solution)/shard_map/stack | solution.py:365
  10.1 5.1 %collective-permute-start.12 = (bf16[3,1808,128]{2,1,0:T(8,128)(2,1)}, bf16[3,1808,128]{2,1,0:T(8,128)(2,1)S(1)}, u32[]{:S(2)}, u32[]{:S(2)}) collective-permute-start(bf16[3,1808,128]{2,1,0:T(8,128)(2,1)} %pad_maximum_fusion), channel_id=1, source_target_pairs={{0,1},{1,2},{2,3},{4,5},{5,6},{6,7},{8,9},{9,10},{10,11},{12,13},{... | collective-permute-start | bytes 4165640 | tf_op jit(solution)/shard_map/ppermute | solution.py:341
  19.1 2.4 %pack_0.1 = (bf16[1808,128]{1,0:T(8,128)(2,1)}, bf16[1808,128]{1,0:T(8,128)(2,1)}) custom-call(s32[1]{0:T(128)} %bitcast.place_ref, bf16[4,4,128,512]{3,2,1,0:T(8,128)(2,1)} %diag_ref.7, bf16[4,4,64,512]{3,2,1,0:T(8,128)(2,1)} %below_ref.7), custom_call_target="tpu_custom_call" | custom-call | bytes 1851392 | tf_op jit(solution)/shard_map/pack_0/pallas_call | solution.py:126
  23.0 9.3 %all-gather = s32[24,4,257]{2,1,0:T(4,128)S(1)} all-gather(s32[3,4,257]{2,1,0:T(4,128)S(1)} %pad_add_fusion), channel_id=2, replica_groups=mesh['leaf'=8,'col'=4] {'leaf'}, dimensions={0}, use_global_device_ids=true | all-gather | bytes 111024 | tf_op jit(solution)/shard_map/all_gather | solution.py:378
  33.8 1.7 slice_bitcast_fusion.8
  37.6 21.6 %collective-permute-done.left0 = bf16[1808,128]{1,0:T(8,128)(2,1)S(1)} collective-permute-done((bf16[1808,128]{1,0:T(8,128)(2,1)}, bf16[1808,128]{1,0:T(8,128)(2,1)S(1)}, u32[]{:S(2)}, u32[]{:S(2)}) %collective-permute-start) | collective-permute-done | bytes 462880 | tf_op jit(solution)/shard_map/ppermute | solution.py:341
  59.1 3.4 %collective-permute-start.4 = (bf16[1,1808,128]{2,1,0:T(8,128)(2,1)}, bf16[1,1808,128]{2,1,0:T(8,128)(2,1)S(1)}, u32[]{:S(2)}, u32[]{:S(2)}) collective-permute-start(bf16[1,1808,128]{2,1,0:T(8,128)(2,1)} %bitcast.16), channel_id=1, source_target_pairs={{0,1},{1,2},{2,3},{4,5},{5,6},{6,7},{8,9},{9,10},{10,11},{12,13},{... | collective-permute-start | bytes 1388552 | tf_op jit(solution)/shard_map/ppermute | solution.py:341
  66.3 5.2 %collective-permute-done.4.right0 = bf16[1,1808,128]{2,1,0:T(8,128)(2,1)S(1)} collective-permute-done((bf16[1,1808,128]{2,1,0:T(8,128)(2,1)}, bf16[1,1808,128]{2,1,0:T(8,128)(2,1)S(1)}, u32[]{:S(2)}, u32[]{:S(2)}) %collective-permute-start.4) | collective-permute-done | bytes 462880 | tf_op jit(solution)/shard_map/ppermute | solution.py:341
  75.6 5.5 %collective-permute-done.1.left1 = bf16[1808,128]{1,0:T(8,128)(2,1)S(1)} collective-permute-done((bf16[1808,128]{1,0:T(8,128)(2,1)S(1)}, bf16[1808,128]{1,0:T(8,128)(2,1)S(1)}, u32[]{:S(2)}, u32[]{:S(2)}) %collective-permute-start.1) | collective-permute-done | bytes 462880 | tf_op jit(solution)/shard_map/ppermute | solution.py:341
  84.6 6.5 %collective-permute-done.9.left1 = bf16[1808,128]{1,0:T(8,128)(2,1)} collective-permute-done((bf16[1808,128]{1,0:T(8,128)(2,1)S(1)}, bf16[1808,128]{1,0:T(8,128)(2,1)}, u32[]{:S(2)}, u32[]{:S(2)}) %collective-permute-start.9) | collective-permute-done | bytes 462880 | tf_op jit(solution)/shard_map/ppermute | solution.py:341
  95.1 31.1 %collective-permute-done.2.left2 = bf16[1808,128]{1,0:T(8,128)(2,1)} collective-permute-done((bf16[1808,128]{1,0:T(8,128)(2,1)S(1)}, bf16[1808,128]{1,0:T(8,128)(2,1)}, u32[]{:S(2)}, u32[]{:S(2)}) %collective-permute-start.2) | collective-permute-done | bytes 462880 | tf_op jit(solution)/shard_map/ppermute | solution.py:341
  126.2 1.8 collective-permute-start.14
  132.1 4.0 %collective-permute-done.10.left2 = bf16[1808,128]{1,0:T(8,128)(2,1)} collective-permute-done((bf16[1808,128]{1,0:T(8,128)(2,1)}, bf16[1808,128]{1,0:T(8,128)(2,1)}, u32[]{:S(2)}, u32[]{:S(2)}) %collective-permute-start.10) | collective-permute-done | bytes 462880 | tf_op jit(solution)/shard_map/ppermute | solution.py:341
  138.4 6.0 %collective-permute-done.3.left3 = bf16[1536,128]{1,0:T(8,128)(2,1)S(1)} collective-permute-done((bf16[1536,128]{1,0:T(8,128)(2,1)S(1)}, bf16[1536,128]{1,0:T(8,128)(2,1)S(1)}, u32[]{:S(2)}, u32[]{:S(2)}) %collective-permute-start.3) | collective-permute-done | bytes 393248 | tf_op jit(solution)/shard_map/ppermute | solution.py:341
  144.5 2.2 %copy-done = bf16[4,4,256,512]{3,2,1,0:T(8,128)(2,1)S(1)} copy-done((bf16[4,4,256,512]{3,2,1,0:T(8,128)(2,1)S(1)}, bf16[4,4,256,512]{3,2,1,0:T(8,128)(2,1)}, u32[]{:S(2)}) %copy-start) | copy-done | bytes 4194328
  147.7 3.9 %solve_0.1 = (bf16[4,4,256,512]{3,2,1,0:T(8,128)(2,1)}, bf16[4,256,256]{2,1,0:T(8,128)(2,1)S(1)}) custom-call(s32[1]{0:T(128)} %bitcast.place_ref, bf16[16,256,512]{2,1,0:T(8,128)(2,1)S(1)} %bitcast.40, bf16[1808,128]{1,0:T(8,128)(2,1)} %get-tuple-element.16.base, bf16[1808,128]{1,0:T(8,128)(2,1)S(1)} %copy-done.13, bf16[1808,128]{1,0:T(8,128)(2,1)S(1)} %copy-done.5, ...), custom_call_target="tpu_custom_call" | custom-call | flops 805306368 | bytes 3145728 | tf_op jit(solution)/shard_map/solve_0/pallas_call | solution.py:305
  154.1 2.4 %source_1.1.source_ref = bf16[4,256,512]{2,1,0:T(8,128)(2,1)S(1)} custom-call(s32[8]{0:T(128)S(1)} %and_select_fusion.1.slots_ref, bf16[4,4,256,512]{3,2,1,0:T(8,128)(2,1)S(1)} %copy-done.1, bf16[4,256,256]{2,1,0:T(8,128)(2,1)S(1)} %get-tuple-element.18.own_ref, bf16[4,256,256]{2,1,0:T(8,128)(2,1)S(1)} %collective-permute-done.7.peer_ref, ...), custom_call_target="tpu_custom_call" | custom-call | flops 536870912 | bytes 3145728 | tf_op jit(solution)/shard_map/source_1/pallas_call | solution.py:167
  156.5 5.1 %collective-permute-done.11.left3 = bf16[1536,128]{1,0:T(8,128)(2,1)S(1)} collective-permute-done((bf16[1536,128]{1,0:T(8,128)(2,1)S(1)}, bf16[1536,128]{1,0:T(8,128)(2,1)S(1)}, u32[]{:S(2)}, u32[]{:S(2)}) %collective-permute-start.11) | collective-permute-done | bytes 393248 | tf_op jit(solution)/shard_map/ppermute | solution.py:341
  161.6 3.9 %solve_1.1 = (bf16[4,4,256,512]{3,2,1,0:T(8,128)(2,1)}, bf16[4,256,256]{2,1,0:T(8,128)(2,1)}) custom-call(s32[1]{0:T(128)} %bitcast.place_ref, bf16[4,256,512]{2,1,0:T(8,128)(2,1)S(1)} %source_1.1.source_ref, bf16[1808,128]{1,0:T(8,128)(2,1)} %get-tuple-element.19.base, bf16[1808,128]{1,0:T(8,128)(2,1)S(1)} %copy-done.11, ...), custom_call_target="tpu_custom_call", output_to_operand_aliasing={{0}: (11, {})} | custom-call | flops 805306368 | bytes 3145728 | tf_op jit(solution)/shard_map/solve_1/pallas_call | solution.py:305
  172.7 2.4 %collective-permute-done.15.peer_ref = bf16[4,256,256]{2,1,0:T(8,128)(2,1)} collective-permute-done((bf16[4,256,256]{2,1,0:T(8,128)(2,1)}, bf16[4,256,256]{2,1,0:T(8,128)(2,1)}, u32[]{:S(2)}, u32[]{:S(2)}) %collective-permute-start.15) | collective-permute-done | bytes 524320 | tf_op jit(solution)/shard_map/ppermute | solution.py:398
  175.1 2.2 %copy-done.2 = bf16[4,4,256,512]{3,2,1,0:T(8,128)(2,1)S(1)} copy-done((bf16[4,4,256,512]{3,2,1,0:T(8,128)(2,1)S(1)}, bf16[4,4,256,512]{3,2,1,0:T(8,128)(2,1)}, u32[]{:S(2)}) %copy-start.2) | copy-done | bytes 4194328
  177.3 3.1 %source_2.1.source_ref = bf16[4,256,512]{2,1,0:T(8,128)(2,1)S(1)} custom-call(s32[8]{0:T(128)S(1)} %and_select_fusion.4.slots_ref, bf16[4,4,256,512]{3,2,1,0:T(8,128)(2,1)S(1)} %copy-done.2, bf16[4,256,256]{2,1,0:T(8,128)(2,1)} %get-tuple-element.26.own_ref, bf16[4,256,256]{2,1,0:T(8,128)(2,1)} %collective-permute-done.15.peer_ref, ...), custom_call_target="tpu_custom_call" | custom-call | flops 536870912 | bytes 3145728 | tf_op jit(solution)/shard_map/source_2/pallas_call | solution.py:167
  180.3 2.6 %collective-permute-done.19.left3 = bf16[1536,128]{1,0:T(8,128)(2,1)} collective-permute-done((bf16[1536,128]{1,0:T(8,128)(2,1)}, bf16[1536,128]{1,0:T(8,128)(2,1)}, u32[]{:S(2)}, u32[]{:S(2)}) %collective-permute-start.19) | collective-permute-done | bytes 393248 | tf_op jit(solution)/shard_map/ppermute | solution.py:341
  183.0 4.0 %solve_2.1 = (bf16[4,4,256,512]{3,2,1,0:T(8,128)(2,1)}, bf16[4,256,256]{2,1,0:T(8,128)(2,1)}) custom-call(s32[1]{0:T(128)} %bitcast.place_ref, bf16[4,256,512]{2,1,0:T(8,128)(2,1)S(1)} %source_2.1.source_ref, bf16[1808,128]{1,0:T(8,128)(2,1)} %get-tuple-element.21.base, bf16[1808,128]{1,0:T(8,128)(2,1)S(1)} %copy-done.9, ...), custom_call_target="tpu_custom_call", output_to_operand_aliasing={{0}: (11, {})} | custom-call | flops 805306368 | bytes 3145728 | tf_op jit(solution)/shard_map/solve_2/pallas_call | solution.py:305
  188.5 1.8 slice.139
  192.1 4.4 %collective-permute-done.20.peer_ref = bf16[4,256,256]{2,1,0:T(8,128)(2,1)} collective-permute-done((bf16[4,256,256]{2,1,0:T(8,128)(2,1)}, bf16[4,256,256]{2,1,0:T(8,128)(2,1)}, u32[]{:S(2)}, u32[]{:S(2)}) %collective-permute-start.20) | collective-permute-done | bytes 524320 | tf_op jit(solution)/shard_map/ppermute | solution.py:398
  196.5 2.2 %copy-done.3 = bf16[4,4,256,512]{3,2,1,0:T(8,128)(2,1)S(1)} copy-done((bf16[4,4,256,512]{3,2,1,0:T(8,128)(2,1)S(1)}, bf16[4,4,256,512]{3,2,1,0:T(8,128)(2,1)}, u32[]{:S(2)}) %copy-start.3) | copy-done | bytes 4194328
  198.7 1.8 source_3.1.source_ref
  200.5 4.0 %solve_3.1 = (bf16[4,4,256,512]{3,2,1,0:T(8,128)(2,1)}, bf16[4,256,256]{2,1,0:T(8,128)(2,1)}) custom-call(s32[1]{0:T(128)} %bitcast.place_ref, bf16[4,256,512]{2,1,0:T(8,128)(2,1)S(1)} %source_3.1.source_ref, bf16[1808,128]{1,0:T(8,128)(2,1)} %get-tuple-element.22.base, bf16[1808,128]{1,0:T(8,128)(2,1)S(1)} %copy-done.7, ...), custom_call_target="tpu_custom_call", output_to_operand_aliasing={{0}: (11, {})} | custom-call | flops 805306368 | bytes 3145728 | tf_op jit(solution)/shard_map/solve_3/pallas_call | solution.py:305
  (128 shorter events, 44.5 us)
Async XLA Ops:
  10.1 52.5 %collective-permute-start.12 = (bf16[3,1808,128]{2,1,0:T(8,128)(2,1)}, bf16[3,1808,128]{2,1,0:T(8,128)(2,1)S(1)}, u32[]{:S(2)}, u32[]{:S(2)}) collective-permute-start(bf16[3,1808,128]{2,1,0:T(8,128)(2,1)} %pad_maximum_fusion), channel_id=1, source_target_pairs={{0,1},{1,2},{2,3},{4,5},{5,6},{6,7},{8,9},{9,10},{10,11},{12,13},{... | collective-permute-start | bytes 4165640 | tf_op jit(solution)/shard_map/ppermute | solution.py:341
  15.2 48.6 %collective-permute-start.8 = (bf16[1808,128]{1,0:T(8,128)(2,1)}, bf16[1808,128]{1,0:T(8,128)(2,1)}, u32[]{:S(2)}, u32[]{:S(2)}) collective-permute-start(bf16[1808,128]{1,0:T(8,128)(2,1)} %get-tuple-element.19.base), channel_id=1, source_target_pairs={{1,0},{2,1},{3,2},{5,4},{6,5},{7,6},{9,8},{10,9},{11,10},{13,12},{... | collective-permute-start | bytes 1388552 | tf_op jit(solution)/shard_map/ppermute | solution.py:341
  16.5 56.3 %collective-permute-start.16 = (bf16[1808,128]{1,0:T(8,128)(2,1)}, bf16[1808,128]{1,0:T(8,128)(2,1)}, u32[]{:S(2)}, u32[]{:S(2)}) collective-permute-start(bf16[1808,128]{1,0:T(8,128)(2,1)} %get-tuple-element.21.base), channel_id=1, source_target_pairs={{1,0},{2,1},{3,2},{5,4},{6,5},{7,6},{9,8},{10,9},{11,10},{13,12},{... | collective-permute-start | bytes 1388552 | tf_op jit(solution)/shard_map/ppermute | solution.py:341
  17.8 111.6 %collective-permute-start.21 = (bf16[1808,128]{1,0:T(8,128)(2,1)}, bf16[1808,128]{1,0:T(8,128)(2,1)S(1)}, u32[]{:S(2)}, u32[]{:S(2)}) collective-permute-start(bf16[1808,128]{1,0:T(8,128)(2,1)} %get-tuple-element.22.base), channel_id=1, source_target_pairs={{1,0},{2,1},{3,2},{5,4},{6,5},{7,6},{9,8},{10,9},{11,10},{13,12},{... | collective-permute-start | bytes 1388552 | tf_op jit(solution)/shard_map/ppermute | solution.py:341
  21.5 37.7 %collective-permute-start = (bf16[1808,128]{1,0:T(8,128)(2,1)}, bf16[1808,128]{1,0:T(8,128)(2,1)S(1)}, u32[]{:S(2)}, u32[]{:S(2)}) collective-permute-start(bf16[1808,128]{1,0:T(8,128)(2,1)} %get-tuple-element.16.base), channel_id=1, source_target_pairs={{1,0},{2,1},{3,2},{5,4},{6,5},{7,6},{9,8},{10,9},{11,10},{13,12},{... | collective-permute-start | bytes 1388552 | tf_op jit(solution)/shard_map/ppermute | solution.py:341
  35.6 27.9 %copy-start.12 = (bf16[1808,128]{1,0:T(8,128)(2,1)S(1)}, bf16[1808,128]{1,0:T(8,128)(2,1)}, u32[]{:S(2)}) copy-start(bf16[1808,128]{1,0:T(8,128)(2,1)} %get-tuple-element.17.rest) | copy-start | bytes 1388548
  35.6 27.9 %copy-start.23 = (bf16[512,128]{1,0:T(8,128)(2,1)S(1)}, bf16[512,128]{1,0:T(8,128)(2,1)}, u32[]{:S(2)}) copy-start(bf16[512,128]{1,0:T(8,128)(2,1)} %get-tuple-element.37) | copy-start | bytes 393220
  59.1 12.4 %collective-permute-start.4 = (bf16[1,1808,128]{2,1,0:T(8,128)(2,1)}, bf16[1,1808,128]{2,1,0:T(8,128)(2,1)S(1)}, u32[]{:S(2)}, u32[]{:S(2)}) collective-permute-start(bf16[1,1808,128]{2,1,0:T(8,128)(2,1)} %bitcast.16), channel_id=1, source_target_pairs={{0,1},{1,2},{2,3},{4,5},{5,6},{6,7},{8,9},{9,10},{10,11},{12,13},{... | collective-permute-start | bytes 1388552 | tf_op jit(solution)/shard_map/ppermute | solution.py:341
  62.6 29.9 %collective-permute-start.13 = (bf16[3,1808,128]{2,1,0:T(8,128)(2,1)S(1)}, bf16[3,1808,128]{2,1,0:T(8,128)(2,1)S(1)}, u32[]{:S(2)}, u32[]{:S(2)}) collective-permute-start(bf16[3,1808,128]{2,1,0:T(8,128)(2,1)S(1)} %collective-permute-done.12.right0), channel_id=1, source_target_pairs={{1,2},{2,3},{5,6},{6,7},{9,10},{10,11},{13,14},{14,15},{17,18},{18... | collective-permute-start | bytes 4165640 | tf_op jit(solution)/shard_map/ppermute | solution.py:341
  63.8 17.3 %collective-permute-start.1 = (bf16[1808,128]{1,0:T(8,128)(2,1)S(1)}, bf16[1808,128]{1,0:T(8,128)(2,1)S(1)}, u32[]{:S(2)}, u32[]{:S(2)}) collective-permute-start(bf16[1808,128]{1,0:T(8,128)(2,1)S(1)} %fusion), channel_id=1, source_target_pairs={{1,0},{2,1},{3,2},{5,4},{6,5},{7,6},{9,8},{10,9},{11,10},{13,12},{... | collective-permute-start | bytes 1388552 | tf_op jit(solution)/shard_map/ppermute | solution.py:341
  71.5 19.6 %collective-permute-start.9 = (bf16[1808,128]{1,0:T(8,128)(2,1)S(1)}, bf16[1808,128]{1,0:T(8,128)(2,1)}, u32[]{:S(2)}, u32[]{:S(2)}) collective-permute-start(bf16[1808,128]{1,0:T(8,128)(2,1)S(1)} %fusion.1), channel_id=1, source_target_pairs={{1,0},{2,1},{3,2},{5,4},{6,5},{7,6},{9,8},{10,9},{11,10},{13,12},{... | collective-permute-start | bytes 1388552 | tf_op jit(solution)/shard_map/ppermute | solution.py:341
  72.8 9.6 %collective-permute-start.5 = (bf16[1,1808,128]{2,1,0:T(8,128)(2,1)S(1)}, bf16[1,1808,128]{2,1,0:T(8,128)(2,1)S(1)}, u32[]{:S(2)}, u32[]{:S(2)}) collective-permute-start(bf16[1,1808,128]{2,1,0:T(8,128)(2,1)S(1)} %collective-permute-done.4.right0), channel_id=1, source_target_pairs={{1,2},{2,3},{5,6},{6,7},{9,10},{10,11},{13,14},{14,15},{17,18},{18... | collective-permute-start | bytes 1388552 | tf_op jit(solution)/shard_map/ppermute | solution.py:341
  81.1 12.8 %copy-start.20 = (bf16[1808,128]{1,0:T(8,128)(2,1)}, bf16[1808,128]{1,0:T(8,128)(2,1)S(1)}, u32[]{:S(2)}) copy-start(bf16[1808,128]{1,0:T(8,128)(2,1)S(1)} %collective-permute-done.1.left1) | copy-start | bytes 1388548
  81.1 49.7 %collective-permute-start.17 = (bf16[1808,128]{1,0:T(8,128)(2,1)}, bf16[1808,128]{1,0:T(8,128)(2,1)}, u32[]{:S(2)}, u32[]{:S(2)}) collective-permute-start(bf16[1808,128]{1,0:T(8,128)(2,1)} %fusion.2), channel_id=1, source_target_pairs={{1,0},{2,1},{3,2},{5,4},{6,5},{7,6},{9,8},{10,9},{11,10},{13,12},{... | collective-permute-start | bytes 1388552 | tf_op jit(solution)/shard_map/ppermute | solution.py:341
  82.4 43.8 %collective-permute-start.2 = (bf16[1808,128]{1,0:T(8,128)(2,1)S(1)}, bf16[1808,128]{1,0:T(8,128)(2,1)}, u32[]{:S(2)}, u32[]{:S(2)}) collective-permute-start(bf16[1808,128]{1,0:T(8,128)(2,1)S(1)} %collective-permute-done.1.left1), channel_id=1, source_target_pairs={{1,0},{2,1},{5,4},{6,5},{9,8},{10,9},{13,12},{14,13},{17,16},{18,1... | collective-permute-start | bytes 1388552 | tf_op jit(solution)/shard_map/ppermute | solution.py:341
  91.1 47.3 %collective-permute-start.6 = (bf16[1,1808,128]{2,1,0:T(8,128)(2,1)}, bf16[1,1808,128]{2,1,0:T(8,128)(2,1)}, u32[]{:S(2)}, u32[]{:S(2)}) collective-permute-start(bf16[1,1808,128]{2,1,0:T(8,128)(2,1)} %pad_maximum_fusion.2), channel_id=1, source_target_pairs={{2,3},{6,7},{10,11},{14,15},{18,19},{22,23},{26,27},{30,31}} | collective-permute-start | bytes 1388552 | tf_op jit(solution)/shard_map/ppermute | solution.py:341
  92.5 43.6 %collective-permute-start.10 = (bf16[1808,128]{1,0:T(8,128)(2,1)}, bf16[1808,128]{1,0:T(8,128)(2,1)}, u32[]{:S(2)}, u32[]{:S(2)}) collective-permute-start(bf16[1808,128]{1,0:T(8,128)(2,1)} %collective-permute-done.9.left1), channel_id=1, source_target_pairs={{1,0},{2,1},{5,4},{6,5},{9,8},{10,9},{13,12},{14,13},{17,16},{18,1... | collective-permute-start | bytes 1388552 | tf_op jit(solution)/shard_map/ppermute | solution.py:341
  126.2 35.4 %collective-permute-start.14 = (bf16[3,1808,128]{2,1,0:T(8,128)(2,1)}, bf16[3,1808,128]{2,1,0:T(8,128)(2,1)}, u32[]{:S(2)}, u32[]{:S(2)}) collective-permute-start(bf16[3,1808,128]{2,1,0:T(8,128)(2,1)} %pad_maximum_fusion.1), channel_id=1, source_target_pairs={{2,3},{6,7},{10,11},{14,15},{18,19},{22,23},{26,27},{30,31}} | collective-permute-start | bytes 4165640 | tf_op jit(solution)/shard_map/ppermute | solution.py:341
  128.3 16.2 %copy-start.5 = (bf16[1808,128]{1,0:T(8,128)(2,1)S(1)}, bf16[1808,128]{1,0:T(8,128)(2,1)}, u32[]{:S(2)}) copy-start(bf16[1808,128]{1,0:T(8,128)(2,1)} %copy-done.4) | copy-start | bytes 1388548
  128.3 16.2 %copy-start.13 = (bf16[1808,128]{1,0:T(8,128)(2,1)S(1)}, bf16[1808,128]{1,0:T(8,128)(2,1)}, u32[]{:S(2)}) copy-start(bf16[1808,128]{1,0:T(8,128)(2,1)} %get-tuple-element.17.rest) | copy-start | bytes 1388548
  128.3 16.2 %copy-start.17 = (bf16[1,1808,128]{2,1,0:T(8,128)(2,1)S(1)}, bf16[1,1808,128]{2,1,0:T(8,128)(2,1)}, u32[]{:S(2)}) copy-start(bf16[1,1808,128]{2,1,0:T(8,128)(2,1)} %copy-done.16) | copy-start | bytes 1388548
  128.3 16.2 %copy-start.19 = (bf16[1,1808,128]{2,1,0:T(8,128)(2,1)S(1)}, bf16[1,1808,128]{2,1,0:T(8,128)(2,1)}, u32[]{:S(2)}) copy-start(bf16[1,1808,128]{2,1,0:T(8,128)(2,1)} %copy-done.18) | copy-start | bytes 1388548
  129.5 15.0 %collective-permute-start.3 = (bf16[1536,128]{1,0:T(8,128)(2,1)S(1)}, bf16[1536,128]{1,0:T(8,128)(2,1)S(1)}, u32[]{:S(2)}, u32[]{:S(2)}) collective-permute-start(bf16[1536,128]{1,0:T(8,128)(2,1)S(1)} %slice.128), channel_id=1, source_target_pairs={{1,0},{5,4},{9,8},{13,12},{17,16},{21,20},{25,24},{29,28}} | collective-permute-start | bytes 1179656 | tf_op jit(solution)/shard_map/ppermute | solution.py:341
  130.8 36.3 %collective-permute-start.18 = (bf16[1808,128]{1,0:T(8,128)(2,1)}, bf16[1808,128]{1,0:T(8,128)(2,1)S(1)}, u32[]{:S(2)}, u32[]{:S(2)}) collective-permute-start(bf16[1808,128]{1,0:T(8,128)(2,1)} %collective-permute-done.17.left1), channel_id=1, source_target_pairs={{1,0},{2,1},{5,4},{6,5},{9,8},{10,9},{13,12},{14,13},{17,16},{18,1... | collective-permute-start | bytes 1388552 | tf_op jit(solution)/shard_map/ppermute | solution.py:341
  137.1 24.5 %collective-permute-start.11 = (bf16[1536,128]{1,0:T(8,128)(2,1)S(1)}, bf16[1536,128]{1,0:T(8,128)(2,1)S(1)}, u32[]{:S(2)}, u32[]{:S(2)}) collective-permute-start(bf16[1536,128]{1,0:T(8,128)(2,1)S(1)} %slice.132), channel_id=1, source_target_pairs={{1,0},{5,4},{9,8},{13,12},{17,16},{21,20},{25,24},{29,28}} | collective-permute-start | bytes 1179656 | tf_op jit(solution)/shard_map/ppermute | solution.py:341
  151.6 2.4 %collective-permute-start.7 = (bf16[4,256,256]{2,1,0:T(8,128)(2,1)S(1)}, bf16[4,256,256]{2,1,0:T(8,128)(2,1)S(1)}, u32[]{:S(2)}, u32[]{:S(2)}) collective-permute-start(bf16[4,256,256]{2,1,0:T(8,128)(2,1)S(1)} %get-tuple-element.18.own_ref), channel_id=1, source_target_pairs={{0,4},{4,0},{8,12},{12,8},{16,20},{20,16},{24,28},{28,24},{1,5},{5... | collective-permute-start | bytes 1572872 | tf_op jit(solution)/shard_map/ppermute | solution.py:398
  152.7 18.4 %collective-permute-start.22 = (bf16[1808,128]{1,0:T(8,128)(2,1)}, bf16[1808,128]{1,0:T(8,128)(2,1)}, u32[]{:S(2)}, u32[]{:S(2)}) collective-permute-start(bf16[1808,128]{1,0:T(8,128)(2,1)} %fusion.3), channel_id=1, source_target_pairs={{1,0},{2,1},{3,2},{5,4},{6,5},{7,6},{9,8},{10,9},{11,10},{13,12},{... | collective-permute-start | bytes 1388552 | tf_op jit(solution)/shard_map/ppermute | solution.py:341
  165.5 9.6 %collective-permute-start.15 = (bf16[4,256,256]{2,1,0:T(8,128)(2,1)}, bf16[4,256,256]{2,1,0:T(8,128)(2,1)}, u32[]{:S(2)}, u32[]{:S(2)}) collective-permute-start(bf16[4,256,256]{2,1,0:T(8,128)(2,1)} %get-tuple-element.26.own_ref), channel_id=1, source_target_pairs={{0,8},{8,0},{4,12},{12,4},{16,24},{24,16},{20,28},{28,20},{1,9},{9... | collective-permute-start | bytes 1572872 | tf_op jit(solution)/shard_map/ppermute | solution.py:398
  168.7 14.2 %collective-permute-start.19 = (bf16[1536,128]{1,0:T(8,128)(2,1)}, bf16[1536,128]{1,0:T(8,128)(2,1)}, u32[]{:S(2)}, u32[]{:S(2)}) collective-permute-start(bf16[1536,128]{1,0:T(8,128)(2,1)} %slice.136), channel_id=1, source_target_pairs={{1,0},{5,4},{9,8},{13,12},{17,16},{21,20},{25,24},{29,28}} | collective-permute-start | bytes 1179656 | tf_op jit(solution)/shard_map/ppermute | solution.py:341
  171.0 17.5 %collective-permute-start.23 = (bf16[1808,128]{1,0:T(8,128)(2,1)}, bf16[1808,128]{1,0:T(8,128)(2,1)}, u32[]{:S(2)}, u32[]{:S(2)}) collective-permute-start(bf16[1808,128]{1,0:T(8,128)(2,1)} %collective-permute-done.22.left1), channel_id=1, source_target_pairs={{1,0},{2,1},{5,4},{6,5},{9,8},{10,9},{13,12},{14,13},{17,16},{18,1... | collective-permute-start | bytes 1388552 | tf_op jit(solution)/shard_map/ppermute | solution.py:341
  186.9 9.6 %collective-permute-start.20 = (bf16[4,256,256]{2,1,0:T(8,128)(2,1)}, bf16[4,256,256]{2,1,0:T(8,128)(2,1)}, u32[]{:S(2)}, u32[]{:S(2)}) collective-permute-start(bf16[4,256,256]{2,1,0:T(8,128)(2,1)} %get-tuple-element.28.own_ref), channel_id=1, source_target_pairs={{0,16},{16,0},{4,20},{20,4},{8,24},{24,8},{12,28},{28,12},{1,17},{... | collective-permute-start | bytes 1572872 | tf_op jit(solution)/shard_map/ppermute | solution.py:398
  190.3 10.2 %collective-permute-start.24 = (bf16[1536,128]{1,0:T(8,128)(2,1)}, bf16[1536,128]{1,0:T(8,128)(2,1)}, u32[]{:S(2)}, u32[]{:S(2)}) collective-permute-start(bf16[1536,128]{1,0:T(8,128)(2,1)} %slice.139), channel_id=1, source_target_pairs={{1,0},{5,4},{9,8},{13,12},{17,16},{21,20},{25,24},{29,28}} | collective-permute-start | bytes 1179656 | tf_op jit(solution)/shard_map/ppermute | solution.py:341
  (20 other events, 117.9 us)

commit v2 on v1

--- a/solution.py
+++ b/solution.py
@@ -7,6 +7,11 @@
 from jax.experimental.pallas import tpu as pltpu
 from jax.sharding import PartitionSpec as P
 
+PLAN = "LR"
+TIE = 0
+TIE_TO = (1,)
+TABLE_TIE = True
+RIGHT_GROUPS = [[0], [1], [2], [3]]
 LANES = 128
 SPARE = 16
 ANY = pl.BlockSpec(memory_space=pl.ANY)
@@ -224,9 +229,22 @@
         def all_off(ref):
             return ref.at[pl.ds(0, 3 * block)]
 
-        r0, r1, r2 = (r.at[group_at] for r in (right0, right1, right2))
+        r0, r1, r2 = (r if PLAN == "SM" else r.at[group_at] for r in (right0, right1, right2))
         second = rest.at[pl.ds(block, block)]
-        where = (
+        if PLAN == "SM":
+            s0, s1, s2, s3, m0, m1, m2 = left0, left1, left2, left3, right0, right1, right2
+            where = (
+                (foot(base), foot(s0), foot(s1), foot(s2),
+                 head(s0), head(s1), head(s2), all_off(s3)),
+                (foot(s0), foot(base), foot(m0), foot(m1),
+                 head(base), head(m0), head(m1), all_off(m2)),
+                (foot(m1), foot(m0), foot(base), foot(s0),
+                 head(m0), head(base), second, all_off(s1)),
+                (foot(s2), foot(s1), foot(s0), foot(base),
+                 head(s1), head(s0), head(s2), all_off(rest)),
+            )
+        else:
+          where = (
             (foot(base), foot(left0), foot(left1), foot(left2),
              head(left0), head(left1), head(left2), all_off(left3)),
             (foot(r0), foot(base), foot(left0), foot(left1),
@@ -349,33 +367,60 @@
     place_ref = place[None]
     up = [(0, 1), (1, 2), (2, 3)]
     down = [(1, 0), (2, 1), (3, 2)]
-    packs = [pack(place_ref, diag_inv, below_panel, t) for t in range(tiers)]
-
-    lefts = []
-    for base, rest in packs:
-        left0 = send(base, down)
-        mixed = jnp.concatenate([rest[block : 2 * block], left0[block:]], 0)
-        left1 = send(jnp.where(place == 1, left0, jnp.where(place == 2, mixed, rest)), down)
-        left2 = send(left1, down[:2])
-        left3 = send(left2[: 3 * block], down[:1])
-        lefts.append((left0, left1, left2, left3))
-
-    rights = []
-    for group in right_groups(tiers):
-        bases = jnp.stack([packs[t][0] for t in group])
-        if group[0] > 0:
-            bases = after(bases, lefts[0][1])
-        right0 = send(bases, up)
-        right1 = send(right0, up[1:])
-        second = jnp.stack([packs[t][1][block : 2 * block] for t in group])
-        right2 = send(jnp.concatenate([second, right1[:, block:]], 1), up[2:])
-        rights += [((right0, right1, right2), i) for i in range(len(group))]
+    packs = []
+    for t in range(tiers):
+        panels = below_panel
+        if t > 0:
+            panels = lax.optimization_barrier((below_panel, packs[t - 1][0]))[0]
+        packs.append(pack(place_ref, diag_inv, panels, t))
+
+    pairs = [(0, 1), (1, 0), (2, 3), (3, 2)]
+    middle = [(1, 2), (2, 1)]
+    lefts, rights = [], []
+    if PLAN == "SM":
+        for t, (base, rest) in enumerate(packs):
+            if TIE and t >= TIE:
+                ref = lefts[t - TIE] + rights[t - TIE][0]
+                base = after(base, *[ref[i] for i in TIE_TO])
+            s0 = send(base, pairs)
+            m0 = send(base, middle)
+            s1 = send(jnp.where(place == 3, rest, m0), pairs)
+            second = jnp.where(place == 2, rest[block : 2 * block], s0[:block])
+            m1 = send(jnp.concatenate([second, s0[block:]], 0), middle)
+            m2 = send(s1[: 3 * block], middle[1:])
+            second = jnp.where(place == 2, rest[block : 2 * block], m1[:block])
+            s2 = send(jnp.concatenate([second, m1[block:]], 0), [(1, 0), (2, 3)])
+            s3 = send(m2, [(1, 0)])
+            lefts.append((s0, s1, s2, s3))
+            rights.append(((m0, m1, m2), 0))
+    else:
+        for t, (base, rest) in enumerate(packs):
+            if TIE and t >= TIE:
+                base = after(base, *[lefts[t - TIE][i] for i in TIE_TO])
+            left0 = send(base, down)
+            mixed = jnp.concatenate([rest[block : 2 * block], left0[block:]], 0)
+            left1 = send(jnp.where(place == 1, left0, jnp.where(place == 2, mixed, rest)), down)
+            left2 = send(left1, down[:2])
+            left3 = send(left2[: 3 * block], down[:1])
+            lefts.append((left0, left1, left2, left3))
+        for group in RIGHT_GROUPS:
+            bases = jnp.stack([packs[t][0] for t in group])
+            if group[0] > 0:
+                bases = after(bases, lefts[group[0] - 1][1])
+            right0 = send(bases, up)
+            right1 = send(right0, up[1:])
+            second = jnp.stack([packs[t][1][block : 2 * block] for t in group])
+            right2 = send(jnp.concatenate([second, right1[:, block:]], 1), up[2:])
+            rights += [((right0, right1, right2), i) for i in range(len(group))]
 
     myself = lax.axis_index("leaf")
     count = lax.axis_size("leaf")
     bit_count = max(count.bit_length() - 1, 1)
     table = jnp.concatenate([parent_map[:, :, None], row_lists], 2)
-    tables = lax.all_gather(table, "leaf")
+    tables = []
+    for t in range(tiers - 1):
+        mine = after(table[t], lefts[0][0]) if TABLE_TIE else table[t]
+        tables.append(lax.ppermute(mine, "leaf", swap_route("leaf", t % bit_count)))
     source, first_block = histograms.reshape(-1, columns, width), 0
     solved = None
     for t in range(tiers):
@@ -397,7 +442,7 @@
         bit = t % bit_count
         peer = lax.ppermute(update, "leaf", swap_route("leaf", bit))
         partner = jnp.bitwise_xor(myself, 1 << bit)
-        theirs = lax.dynamic_index_in_dim(tables, jnp.minimum(partner, count - 1), 0, False)[t]
+        theirs = tables[t]
         parents = jnp.concatenate([parent_map[t], theirs[:, 0]])
         exists = jnp.repeat(jnp.stack([partner >= 0, partner < count]), per_device)
         mine = jnp.logical_and(parents // per_device == myself, exists)
@@ -405,10 +450,6 @@
         source = source_of(histograms, t + 1, update, peer, slots, row_lists[t], theirs[:, 1:])
         first_block = 0
     return solved, update
-
-
-def right_groups(tiers):
-    return [[0], list(range(1, tiers))]
 
 
 def on_device(histograms, diag_inv, below_panel, parent_map, row_lists):

time: 208 us -> 176 us (0.85)
  waiting for transfers between devices: 95.3 us -> 58 us
  starting transfers between devices: 37.1 us -> 55.7 us
  blocking collectives: 9.25 us -> 0 us
  local copies, waits for them, and re-layouts: 21.7 us -> 18.3 us
    ppermute x22 -> x28, waiting for transfers between devices: 88.6 us -> 52.2 us  [send(): return lax.ppermute(value, 'col', route)]
    ppermute x22 -> x28, starting transfers between devices: 33.9 us -> 50.5 us  [send(): return lax.ppermute(value, 'col', route)]
    all_gather x1 -> x0, blocking collectives: 9.25 us -> none  [line_plan(): tables = lax.all_gather(table, 'leaf')]
    slice x4, local copies, waits for them, and re-layouts: 4.76 us -> 0.86 us  [line_plan(): left3 = send(left2[:3 * block], down[:1])]
    ppermute x0 -> x3, starting transfers between devices: none -> 3.09 us  [line_plan(): tables.append(lax.ppermute(mine, 'leaf', swap_route('leaf', t % bit_count)))]
    select_n x4, other arithmetic: 2.46 us -> 5.07 us  [line_plan(): jnp.where(place == 1, left0, jnp.where(place == 2, mixed, rest))]
    another operation x1 -> x0, other arithmetic: 2.53 us -> none  [line_plan(): bases = jnp.stack([packs[t][0] for t in group])]
    another operation x2 -> x4, local copies, waits for them, and re-layouts: 3.26 us -> 5.61 us  [line_plan(): second = jnp.stack([packs[t][1][block:2 * block] for t in group])]
  transfers between devices with their start and end apart: 25 -> 34, of which waited for: 12 -> 10; matrix products, arithmetic and copies ran while one was open for 9% -> 11% of each run, Pallas kernels for 10% -> 15%
where the time goes in v2:
time: 176 us; the launch traced here: 174 us
  waiting for transfers between devices  58 us (33%)
  starting transfers between devices  55.7 us (32%)
  Pallas kernels  32.2 us (18%)
  local copies, waits for them, and re-layouts  18.3 us (10%)
  other arithmetic  8.23 us (5%)
    ppermute x28, waiting for transfers between devices, send(): return lax.ppermute(value, 'col', route)  52.2 us
    ppermute x28, starting transfers between devices, send(): return lax.ppermute(value, 'col', route)  50.5 us
    pallas_call x4, Pallas kernels, solve(): pl.pallas_call(functools.partial(solve_kernel, group_at, has_prior), grid...  16 us
    pallas_call x4, Pallas kernels, pack(): pl.pallas_call(pack_kernel, grid=(1,), in_specs=[SMEM, pl.BlockSpec((1, p...  9.23 us
    unnamed x48, local copies, waits for them, and re-layouts  7.49 us
    pallas_call x3, Pallas kernels, source_of(): pl.pallas_call(source_kernel, grid=(1,), in_specs=[SMEM, pl.BlockSpec((1,...  6.95 us
    ppermute x3, waiting for transfers between devices, line_plan(): peer = lax.ppermute(update, 'leaf', swap_route('leaf', bit))  5.76 us
    another operation x4, local copies, waits for them, and re-layouts, line_plan(): second = jnp.stack([packs[t][1][block:2 * block] for t in group])  5.61 us
  transfers between devices with their start and end apart: 34, of which 10 were waited for; matrix products, arithmetic and copies ran while one was open for 11% of the time, Pallas kernels for 15%

profile of v2, /device:TPU:0, one launch (start us, length us, event | category | flops | bytes accessed | tf_op | source)
XLA Modules:
  0.0 173.8 jit_solution(5959887890716858392)
XLA Ops:
  0.6 2.3 %pack_0.1 = (bf16[1808,128]{1,0:T(8,128)(2,1)}, bf16[1808,128]{1,0:T(8,128)(2,1)}) custom-call(s32[1]{0:T(128)} %bitcast.place_ref, bf16[4,4,128,512]{3,2,1,0:T(8,128)(2,1)} %diag_ref.7, bf16[4,4,64,512]{3,2,1,0:T(8,128)(2,1)} %below_ref.4), custom_call_target="tpu_custom_call" | custom-call | bytes 1851392 | tf_op jit(solution)/shard_map/pack_0/pallas_call | solution.py:131
  4.4 6.3 %collective-permute-start.7 = (bf16[1,1808,128]{2,1,0:T(8,128)(2,1)}, bf16[1,1808,128]{2,1,0:T(8,128)(2,1)}, u32[]{:S(2)}, u32[]{:S(2)}) collective-permute-start(bf16[1,1808,128]{2,1,0:T(8,128)(2,1)} %bitcast.41), channel_id=1, source_target_pairs={{0,1},{1,2},{2,3},{4,5},{5,6},{6,7},{8,9},{9,10},{10,11},{12,13},{... | collective-permute-start | bytes 1388552 | tf_op jit(solution)/shard_map/ppermute | solution.py:359
  10.7 2.3 %pack_1.1 = (bf16[1808,128]{1,0:T(8,128)(2,1)}, bf16[1808,128]{1,0:T(8,128)(2,1)}) custom-call(s32[1]{0:T(128)} %bitcast.place_ref, bf16[4,4,128,512]{3,2,1,0:T(8,128)(2,1)} %diag_ref.7, bf16[4,4,64,512]{3,2,1,0:T(8,128)(2,1)} %below_ref.4), custom_call_target="tpu_custom_call" | custom-call | bytes 1851392 | tf_op jit(solution)/shard_map/pack_1/pallas_call | solution.py:131
  14.3 4.6 %collective-permute-start.15 = (bf16[1,1808,128]{2,1,0:T(8,128)(2,1)}, bf16[1,1808,128]{2,1,0:T(8,128)(2,1)S(1)}, u32[]{:S(2)}, u32[]{:S(2)}) collective-permute-start(bf16[1,1808,128]{2,1,0:T(8,128)(2,1)} %bitcast.40), channel_id=1, source_target_pairs={{0,1},{1,2},{2,3},{4,5},{5,6},{6,7},{8,9},{9,10},{10,11},{12,13},{... | collective-permute-start | bytes 1388552 | tf_op jit(solution)/shard_map/ppermute | solution.py:359
  18.9 2.3 %pack_2.1 = (bf16[1808,128]{1,0:T(8,128)(2,1)}, bf16[1808,128]{1,0:T(8,128)(2,1)}) custom-call(s32[1]{0:T(128)} %bitcast.place_ref, bf16[4,4,128,512]{3,2,1,0:T(8,128)(2,1)} %diag_ref.7, bf16[4,4,64,512]{3,2,1,0:T(8,128)(2,1)} %below_ref.4), custom_call_target="tpu_custom_call" | custom-call | bytes 1851392 | tf_op jit(solution)/shard_map/pack_2/pallas_call | solution.py:131
  24.0 1.6 slice_bitcast_fusion.8
  25.7 2.3 %pack_3.1 = (bf16[1808,128]{1,0:T(8,128)(2,1)}, bf16[1808,128]{1,0:T(8,128)(2,1)}) custom-call(s32[1]{0:T(128)} %bitcast.place_ref, bf16[4,4,128,512]{3,2,1,0:T(8,128)(2,1)} %diag_ref.7, bf16[4,4,64,512]{3,2,1,0:T(8,128)(2,1)} %below_ref.4), custom_call_target="tpu_custom_call" | custom-call | bytes 1851392 | tf_op jit(solution)/shard_map/pack_3/pallas_call | solution.py:131
  28.0 1.6 slice_bitcast_fusion.7
  29.6 1.6 slice_bitcast_fusion.6
  31.2 5.3 %collective-permute-start.23 = (bf16[1,1808,128]{2,1,0:T(8,128)(2,1)}, bf16[1,1808,128]{2,1,0:T(8,128)(2,1)}, u32[]{:S(2)}, u32[]{:S(2)}) collective-permute-start(bf16[1,1808,128]{2,1,0:T(8,128)(2,1)} %bitcast.21), channel_id=1, source_target_pairs={{0,1},{1,2},{2,3},{4,5},{5,6},{6,7},{8,9},{9,10},{10,11},{12,13},{... | collective-permute-start | bytes 1388552 | tf_op jit(solution)/shard_map/ppermute | solution.py:359
  40.5 1.9 %fusion.1 = bf16[1808,128]{1,0:T(8,128)(2,1)} fusion(bf16[1808,128]{1,0:T(8,128)(2,1)S(1)} %collective-permute-done.11.left0, bf16[1808,128]{1,0:T(8,128)(2,1)S(1)} %copy-done.5, bf16[1296,128]{1,0:T(8,128)(2,1)S(1)} %slice.149, bf16[512,128]{1,0:T(8,128)(2,1)} %get-tuple-element.47, pred[]{:T(512)S(6)} %eq.35, pred[]{:T(512)S(6)} %eq.34), kind=kLoop, calls=%fused_computation.4 | loop fusion | flops 1388544 | bytes 1851394 | tf_op jit(solution)/shard_map/jit(_where)/select_n | solution.py:402
  45.0 8.3 %collective-permute-done.4.left1 = bf16[1808,128]{1,0:T(8,128)(2,1)} collective-permute-done((bf16[1808,128]{1,0:T(8,128)(2,1)S(1)}, bf16[1808,128]{1,0:T(8,128)(2,1)}, u32[]{:S(2)}, u32[]{:S(2)}) %collective-permute-start.4) | collective-permute-done | bytes 462880 | tf_op jit(solution)/shard_map/ppermute | solution.py:359
  59.0 14.1 %collective-permute-done.12.left1 = bf16[1808,128]{1,0:T(8,128)(2,1)} collective-permute-done((bf16[1808,128]{1,0:T(8,128)(2,1)}, bf16[1808,128]{1,0:T(8,128)(2,1)}, u32[]{:S(2)}, u32[]{:S(2)}) %collective-permute-start.12) | collective-permute-done | bytes 462880 | tf_op jit(solution)/shard_map/ppermute | solution.py:359
  73.8 6.5 %collective-permute-done.5.left2 = bf16[1808,128]{1,0:T(8,128)(2,1)S(1)} collective-permute-done((bf16[1808,128]{1,0:T(8,128)(2,1)}, bf16[1808,128]{1,0:T(8,128)(2,1)S(1)}, u32[]{:S(2)}, u32[]{:S(2)}) %collective-permute-start.5) | collective-permute-done | bytes 462880 | tf_op jit(solution)/shard_map/ppermute | solution.py:359
  84.1 5.4 %collective-permute-start.31 = (bf16[1,1808,128]{2,1,0:T(8,128)(2,1)}, bf16[1,1808,128]{2,1,0:T(8,128)(2,1)}, u32[]{:S(2)}, u32[]{:S(2)}) collective-permute-start(bf16[1,1808,128]{2,1,0:T(8,128)(2,1)} %bitcast.24), channel_id=1, source_target_pairs={{0,1},{1,2},{2,3},{4,5},{5,6},{6,7},{8,9},{9,10},{10,11},{12,13},{... | collective-permute-start | bytes 1388552 | tf_op jit(solution)/shard_map/ppermute | solution.py:359
  89.5 6.4 %collective-permute-done.13.left2 = bf16[1808,128]{1,0:T(8,128)(2,1)S(1)} collective-permute-done((bf16[1808,128]{1,0:T(8,128)(2,1)}, bf16[1808,128]{1,0:T(8,128)(2,1)S(1)}, u32[]{:S(2)}, u32[]{:S(2)}) %collective-permute-start.13) | collective-permute-done | bytes 462880 | tf_op jit(solution)/shard_map/ppermute | solution.py:359
  97.4 3.4 %collective-permute-done.6.left3 = bf16[1536,128]{1,0:T(8,128)(2,1)S(1)} collective-permute-done((bf16[1536,128]{1,0:T(8,128)(2,1)S(1)}, bf16[1536,128]{1,0:T(8,128)(2,1)S(1)}, u32[]{:S(2)}, u32[]{:S(2)}) %collective-permute-start.6) | collective-permute-done | bytes 393248 | tf_op jit(solution)/shard_map/ppermute | solution.py:359
  103.6 3.8 %solve_0.1 = (bf16[4,4,256,512]{3,2,1,0:T(8,128)(2,1)}, bf16[4,256,256]{2,1,0:T(8,128)(2,1)S(1)}) custom-call(s32[1]{0:T(128)} %bitcast.place_ref, bf16[16,256,512]{2,1,0:T(8,128)(2,1)S(1)} %bitcast.39, bf16[1808,128]{1,0:T(8,128)(2,1)S(1)} %copy-done.15, bf16[1808,128]{1,0:T(8,128)(2,1)S(1)} %copy-done.7, bf16[1808,128]{1,0:T(8,128)(2,1)S(1)} %collective-permute-done.left0, ...), custom_call_target="tpu_custom_call" | custom-call | flops 805306368 | bytes 3145728 | tf_op jit(solution)/shard_map/solve_0/pallas_call | solution.py:323
  110.0 1.5 collective-permute-done.20.left1
  112.9 1.7 collective-permute-start.2
  114.6 1.9 %source_1.1.source_ref = bf16[4,256,512]{2,1,0:T(8,128)(2,1)S(1)} custom-call(s32[8]{0:T(128)S(1)} %and_select_fusion.1.slots_ref, bf16[4,4,256,512]{3,2,1,0:T(8,128)(2,1)S(1)} %copy-done, bf16[4,256,256]{2,1,0:T(8,128)(2,1)S(1)} %get-tuple-element.27.own_ref, bf16[4,256,256]{2,1,0:T(8,128)(2,1)S(1)} %collective-permute-done.10.peer_ref, ...), custom_call_target="tpu_custom_call" | custom-call | flops 536870912 | bytes 3145728 | tf_op jit(solution)/shard_map/source_1/pallas_call | solution.py:172
  119.2 2.2 %collective-permute-done.14.left3 = bf16[1536,128]{1,0:T(8,128)(2,1)S(1)} collective-permute-done((bf16[1536,128]{1,0:T(8,128)(2,1)S(1)}, bf16[1536,128]{1,0:T(8,128)(2,1)S(1)}, u32[]{:S(2)}, u32[]{:S(2)}) %collective-permute-start.14) | collective-permute-done | bytes 393248 | tf_op jit(solution)/shard_map/ppermute | solution.py:359
  121.4 4.0 %solve_1.1 = (bf16[4,4,256,512]{3,2,1,0:T(8,128)(2,1)}, bf16[4,256,256]{2,1,0:T(8,128)(2,1)}) custom-call(s32[1]{0:T(128)} %bitcast.place_ref, bf16[4,256,512]{2,1,0:T(8,128)(2,1)S(1)} %source_1.1.source_ref, bf16[1808,128]{1,0:T(8,128)(2,1)S(1)} %copy-done.12, bf16[1808,128]{1,0:T(8,128)(2,1)S(1)} %copy-done.5, ...), custom_call_target="tpu_custom_call", output_to_operand_aliasing={{0}: (11, {})} | custom-call | flops 805306368 | bytes 3145728 | tf_op jit(solution)/shard_map/solve_1/pallas_call | solution.py:323
  127.6 3.7 %collective-permute-done.21.left2 = bf16[1808,128]{1,0:T(8,128)(2,1)S(1)} collective-permute-done((bf16[1808,128]{1,0:T(8,128)(2,1)S(1)}, bf16[1808,128]{1,0:T(8,128)(2,1)S(1)}, u32[]{:S(2)}, u32[]{:S(2)}) %collective-permute-start.21) | collective-permute-done | bytes 462880 | tf_op jit(solution)/shard_map/ppermute | solution.py:359
  135.2 6.2 %collective-permute-done.28.left1 = bf16[1808,128]{1,0:T(8,128)(2,1)} collective-permute-done((bf16[1808,128]{1,0:T(8,128)(2,1)}, bf16[1808,128]{1,0:T(8,128)(2,1)}, u32[]{:S(2)}, u32[]{:S(2)}) %collective-permute-start.28) | collective-permute-done | bytes 462880 | tf_op jit(solution)/shard_map/ppermute | solution.py:359
  145.2 2.2 %copy-done.1 = bf16[4,4,256,512]{3,2,1,0:T(8,128)(2,1)S(1)} copy-done((bf16[4,4,256,512]{3,2,1,0:T(8,128)(2,1)S(1)}, bf16[4,4,256,512]{3,2,1,0:T(8,128)(2,1)}, u32[]{:S(2)}) %copy-start.1) | copy-done | bytes 4194328
  147.4 3.2 %source_2.1.source_ref = bf16[4,256,512]{2,1,0:T(8,128)(2,1)S(1)} custom-call(s32[8]{0:T(128)S(1)} %and_select_fusion.4.slots_ref, bf16[4,4,256,512]{3,2,1,0:T(8,128)(2,1)S(1)} %copy-done.1, bf16[4,256,256]{2,1,0:T(8,128)(2,1)} %get-tuple-element.32.own_ref, bf16[4,256,256]{2,1,0:T(8,128)(2,1)} %collective-permute-done.18.peer_ref, ...), custom_call_target="tpu_custom_call" | custom-call | flops 536870912 | bytes 3145728 | tf_op jit(solution)/shard_map/source_2/pallas_call | solution.py:172
  151.7 4.3 %solve_2.1 = (bf16[4,4,256,512]{3,2,1,0:T(8,128)(2,1)}, bf16[4,256,256]{2,1,0:T(8,128)(2,1)}) custom-call(s32[1]{0:T(128)} %bitcast.place_ref, bf16[4,256,512]{2,1,0:T(8,128)(2,1)S(1)} %source_2.1.source_ref, bf16[1808,128]{1,0:T(8,128)(2,1)} %get-tuple-element.34.base, bf16[1808,128]{1,0:T(8,128)(2,1)S(1)} %copy-done.4, ...), custom_call_target="tpu_custom_call", output_to_operand_aliasing={{0}: (11, {})} | custom-call | flops 805306368 | bytes 3145728 | tf_op jit(solution)/shard_map/solve_2/pallas_call | solution.py:323
  160.0 5.8 %collective-permute-done.26.peer_ref = bf16[4,256,256]{2,1,0:T(8,128)(2,1)S(1)} collective-permute-done((bf16[4,256,256]{2,1,0:T(8,128)(2,1)}, bf16[4,256,256]{2,1,0:T(8,128)(2,1)S(1)}, u32[]{:S(2)}, u32[]{:S(2)}) %collective-permute-start.26) | collective-permute-done | bytes 524320 | tf_op jit(solution)/shard_map/ppermute | solution.py:443
  165.7 2.2 %copy-done.2 = bf16[4,4,256,512]{3,2,1,0:T(8,128)(2,1)S(1)} copy-done((bf16[4,4,256,512]{3,2,1,0:T(8,128)(2,1)S(1)}, bf16[4,4,256,512]{3,2,1,0:T(8,128)(2,1)}, u32[]{:S(2)}) %copy-start.2) | copy-done | bytes 4194328
  167.9 1.9 %source_3.1.source_ref = bf16[4,256,512]{2,1,0:T(8,128)(2,1)S(1)} custom-call(s32[8]{0:T(128)S(1)} %and_select_fusion.7.slots_ref, bf16[4,4,256,512]{3,2,1,0:T(8,128)(2,1)S(1)} %copy-done.2, bf16[4,256,256]{2,1,0:T(8,128)(2,1)} %get-tuple-element.37.own_ref, bf16[4,256,256]{2,1,0:T(8,128)(2,1)S(1)} %collective-permute-done.26.peer_ref, ...), custom_call_target="tpu_custom_call" | custom-call | flops 536870912 | bytes 3145728 | tf_op jit(solution)/shard_map/source_3/pallas_call | solution.py:172
  169.8 3.9 %solve_3.1 = (bf16[4,4,256,512]{3,2,1,0:T(8,128)(2,1)}, bf16[4,256,256]{2,1,0:T(8,128)(2,1)}) custom-call(s32[1]{0:T(128)} %bitcast.place_ref, bf16[4,256,512]{2,1,0:T(8,128)(2,1)S(1)} %source_3.1.source_ref, bf16[1808,128]{1,0:T(8,128)(2,1)} %get-tuple-element.39.base, bf16[1808,128]{1,0:T(8,128)(2,1)S(1)} %copy-done.3, ...), custom_call_target="tpu_custom_call", output_to_operand_aliasing={{0}: (11, {})} | custom-call | flops 805306368 | bytes 3145728 | tf_op jit(solution)/shard_map/solve_3/pallas_call | solution.py:323
  (142 shorter events, 47.9 us)
Async XLA Ops:
  2.9 28.3 %collective-permute-start = (bf16[1808,128]{1,0:T(8,128)(2,1)}, bf16[1808,128]{1,0:T(8,128)(2,1)S(1)}, u32[]{:S(2)}, u32[]{:S(2)}) collective-permute-start(bf16[1808,128]{1,0:T(8,128)(2,1)} %get-tuple-element.22.base), channel_id=1, source_target_pairs={{1,0},{2,1},{3,2},{5,4},{6,5},{7,6},{9,8},{10,9},{11,10},{13,12},{... | collective-permute-start | bytes 1388552 | tf_op jit(solution)/shard_map/ppermute | solution.py:359
  4.4 33.3 %collective-permute-start.7 = (bf16[1,1808,128]{2,1,0:T(8,128)(2,1)}, bf16[1,1808,128]{2,1,0:T(8,128)(2,1)}, u32[]{:S(2)}, u32[]{:S(2)}) collective-permute-start(bf16[1,1808,128]{2,1,0:T(8,128)(2,1)} %bitcast.41), channel_id=1, source_target_pairs={{0,1},{1,2},{2,3},{4,5},{5,6},{6,7},{8,9},{9,10},{10,11},{12,13},{... | collective-permute-start | bytes 1388552 | tf_op jit(solution)/shard_map/ppermute | solution.py:359
  13.0 26.0 %collective-permute-start.11 = (bf16[1808,128]{1,0:T(8,128)(2,1)}, bf16[1808,128]{1,0:T(8,128)(2,1)S(1)}, u32[]{:S(2)}, u32[]{:S(2)}) collective-permute-start(bf16[1808,128]{1,0:T(8,128)(2,1)} %get-tuple-element.29.base), channel_id=1, source_target_pairs={{1,0},{2,1},{3,2},{5,4},{6,5},{7,6},{9,8},{10,9},{11,10},{13,12},{... | collective-permute-start | bytes 1388552 | tf_op jit(solution)/shard_map/ppermute | solution.py:359
  14.3 28.1 %collective-permute-start.15 = (bf16[1,1808,128]{2,1,0:T(8,128)(2,1)}, bf16[1,1808,128]{2,1,0:T(8,128)(2,1)S(1)}, u32[]{:S(2)}, u32[]{:S(2)}) collective-permute-start(bf16[1,1808,128]{2,1,0:T(8,128)(2,1)} %bitcast.40), channel_id=1, source_target_pairs={{0,1},{1,2},{2,3},{4,5},{5,6},{6,7},{8,9},{9,10},{10,11},{12,13},{... | collective-permute-start | bytes 1388552 | tf_op jit(solution)/shard_map/ppermute | solution.py:359
  21.2 22.5 %collective-permute-start.19 = (bf16[1808,128]{1,0:T(8,128)(2,1)}, bf16[1808,128]{1,0:T(8,128)(2,1)S(1)}, u32[]{:S(2)}, u32[]{:S(2)}) collective-permute-start(bf16[1808,128]{1,0:T(8,128)(2,1)} %get-tuple-element.34.base), channel_id=1, source_target_pairs={{1,0},{2,1},{3,2},{5,4},{6,5},{7,6},{9,8},{10,9},{11,10},{13,12},{... | collective-permute-start | bytes 1388552 | tf_op jit(solution)/shard_map/ppermute | solution.py:359
  31.2 24.1 %collective-permute-start.23 = (bf16[1,1808,128]{2,1,0:T(8,128)(2,1)}, bf16[1,1808,128]{2,1,0:T(8,128)(2,1)}, u32[]{:S(2)}, u32[]{:S(2)}) collective-permute-start(bf16[1,1808,128]{2,1,0:T(8,128)(2,1)} %bitcast.21), channel_id=1, source_target_pairs={{0,1},{1,2},{2,3},{4,5},{5,6},{6,7},{8,9},{9,10},{10,11},{12,13},{... | collective-permute-start | bytes 1388552 | tf_op jit(solution)/shard_map/ppermute | solution.py:359
  37.7 15.5 %collective-permute-start.4 = (bf16[1808,128]{1,0:T(8,128)(2,1)S(1)}, bf16[1808,128]{1,0:T(8,128)(2,1)}, u32[]{:S(2)}, u32[]{:S(2)}) collective-permute-start(bf16[1808,128]{1,0:T(8,128)(2,1)S(1)} %fusion), channel_id=1, source_target_pairs={{1,0},{2,1},{3,2},{5,4},{6,5},{7,6},{9,8},{10,9},{11,10},{13,12},{... | collective-permute-start | bytes 1388552 | tf_op jit(solution)/shard_map/ppermute | solution.py:359
  39.0 17.2 %collective-permute-start.8 = (bf16[1,1808,128]{2,1,0:T(8,128)(2,1)}, bf16[1,1808,128]{2,1,0:T(8,128)(2,1)}, u32[]{:S(2)}, u32[]{:S(2)}) collective-permute-start(bf16[1,1808,128]{2,1,0:T(8,128)(2,1)} %collective-permute-done.7.right0), channel_id=1, source_target_pairs={{1,2},{2,3},{5,6},{6,7},{9,10},{10,11},{13,14},{14,15},{17,18},{18... | collective-permute-start | bytes 1388552 | tf_op jit(solution)/shard_map/ppermute | solution.py:359
  42.4 39.2 %collective-permute-start.27 = (bf16[1808,128]{1,0:T(8,128)(2,1)}, bf16[1808,128]{1,0:T(8,128)(2,1)S(1)}, u32[]{:S(2)}, u32[]{:S(2)}) collective-permute-start(bf16[1808,128]{1,0:T(8,128)(2,1)} %get-tuple-element.39.base), channel_id=1, source_target_pairs={{1,0},{2,1},{3,2},{5,4},{6,5},{7,6},{9,8},{10,9},{11,10},{13,12},{... | collective-permute-start | bytes 1388552 | tf_op jit(solution)/shard_map/ppermute | solution.py:359
  43.7 29.4 %collective-permute-start.12 = (bf16[1808,128]{1,0:T(8,128)(2,1)}, bf16[1808,128]{1,0:T(8,128)(2,1)}, u32[]{:S(2)}, u32[]{:S(2)}) collective-permute-start(bf16[1808,128]{1,0:T(8,128)(2,1)} %fusion.1), channel_id=1, source_target_pairs={{1,0},{2,1},{3,2},{5,4},{6,5},{7,6},{9,8},{10,9},{11,10},{13,12},{... | collective-permute-start | bytes 1388552 | tf_op jit(solution)/shard_map/ppermute | solution.py:359
  53.2 27.1 %collective-permute-start.5 = (bf16[1808,128]{1,0:T(8,128)(2,1)}, bf16[1808,128]{1,0:T(8,128)(2,1)S(1)}, u32[]{:S(2)}, u32[]{:S(2)}) collective-permute-start(bf16[1808,128]{1,0:T(8,128)(2,1)} %collective-permute-done.4.left1), channel_id=1, source_target_pairs={{1,0},{2,1},{5,4},{6,5},{9,8},{10,9},{13,12},{14,13},{17,16},{18,1... | collective-permute-start | bytes 1388552 | tf_op jit(solution)/shard_map/ppermute | solution.py:359
  55.4 28.7 %collective-permute-start.16 = (bf16[1,1808,128]{2,1,0:T(8,128)(2,1)}, bf16[1,1808,128]{2,1,0:T(8,128)(2,1)S(1)}, u32[]{:S(2)}, u32[]{:S(2)}) collective-permute-start(bf16[1,1808,128]{2,1,0:T(8,128)(2,1)} %copy-done.13), channel_id=1, source_target_pairs={{1,2},{2,3},{5,6},{6,7},{9,10},{10,11},{13,14},{14,15},{17,18},{18... | collective-permute-start | bytes 1388552 | tf_op jit(solution)/shard_map/ppermute | solution.py:359
  56.2 52.5 %collective-permute-start.24 = (bf16[1,1808,128]{2,1,0:T(8,128)(2,1)}, bf16[1,1808,128]{2,1,0:T(8,128)(2,1)S(1)}, u32[]{:S(2)}, u32[]{:S(2)}) collective-permute-start(bf16[1,1808,128]{2,1,0:T(8,128)(2,1)} %collective-permute-done.23.right0), channel_id=1, source_target_pairs={{1,2},{2,3},{5,6},{6,7},{9,10},{10,11},{13,14},{14,15},{17,18},{18... | collective-permute-start | bytes 1388552 | tf_op jit(solution)/shard_map/ppermute | solution.py:359
  73.1 22.9 %collective-permute-start.9 = (bf16[1,1808,128]{2,1,0:T(8,128)(2,1)S(1)}, bf16[1,1808,128]{2,1,0:T(8,128)(2,1)S(1)}, u32[]{:S(2)}, u32[]{:S(2)}) collective-permute-start(bf16[1,1808,128]{2,1,0:T(8,128)(2,1)S(1)} %pad_maximum_fusion), channel_id=1, source_target_pairs={{2,3},{6,7},{10,11},{14,15},{18,19},{22,23},{26,27},{30,31}} | collective-permute-start | bytes 1388552 | tf_op jit(solution)/shard_map/ppermute | solution.py:359
  80.3 15.6 %collective-permute-start.13 = (bf16[1808,128]{1,0:T(8,128)(2,1)}, bf16[1808,128]{1,0:T(8,128)(2,1)S(1)}, u32[]{:S(2)}, u32[]{:S(2)}) collective-permute-start(bf16[1808,128]{1,0:T(8,128)(2,1)} %collective-permute-done.12.left1), channel_id=1, source_target_pairs={{1,0},{2,1},{5,4},{6,5},{9,8},{10,9},{13,12},{14,13},{17,16},{18,1... | collective-permute-start | bytes 1388552 | tf_op jit(solution)/shard_map/ppermute | solution.py:359
  81.6 19.2 %collective-permute-start.6 = (bf16[1536,128]{1,0:T(8,128)(2,1)S(1)}, bf16[1536,128]{1,0:T(8,128)(2,1)S(1)}, u32[]{:S(2)}, u32[]{:S(2)}) collective-permute-start(bf16[1536,128]{1,0:T(8,128)(2,1)S(1)} %slice.146), channel_id=1, source_target_pairs={{1,0},{5,4},{9,8},{13,12},{17,16},{21,20},{25,24},{29,28}} | collective-permute-start | bytes 1179656 | tf_op jit(solution)/shard_map/ppermute | solution.py:359
  84.1 32.4 %collective-permute-start.31 = (bf16[1,1808,128]{2,1,0:T(8,128)(2,1)}, bf16[1,1808,128]{2,1,0:T(8,128)(2,1)}, u32[]{:S(2)}, u32[]{:S(2)}) collective-permute-start(bf16[1,1808,128]{2,1,0:T(8,128)(2,1)} %bitcast.24), channel_id=1, source_target_pairs={{0,1},{1,2},{2,3},{4,5},{5,6},{6,7},{8,9},{9,10},{10,11},{12,13},{... | collective-permute-start | bytes 1388552 | tf_op jit(solution)/shard_map/ppermute | solution.py:359
  95.9 11.5 %collective-permute-start.3 = (s32[4,257]{1,0:T(4,128)S(1)}, s32[4,257]{1,0:T(4,128)S(1)}, u32[]{:S(2)}, u32[]{:S(2)}) collective-permute-start(s32[4,257]{1,0:T(4,128)S(1)} %get-tuple-element.25), channel_id=1, source_target_pairs={{0,4},{4,0},{8,12},{12,8},{16,20},{20,16},{24,28},{28,24},{1,5},{5... | collective-permute-start | bytes 12344 | tf_op jit(solution)/shard_map/ppermute | solution.py:423
  96.0 15.4 %collective-permute-start.20 = (bf16[1808,128]{1,0:T(8,128)(2,1)S(1)}, bf16[1808,128]{1,0:T(8,128)(2,1)S(1)}, u32[]{:S(2)}, u32[]{:S(2)}) collective-permute-start(bf16[1808,128]{1,0:T(8,128)(2,1)S(1)} %fusion.2), channel_id=1, source_target_pairs={{1,0},{2,1},{3,2},{5,4},{6,5},{7,6},{9,8},{10,9},{11,10},{13,12},{... | collective-permute-start | bytes 1388552 | tf_op jit(solution)/shard_map/ppermute | solution.py:359
  100.8 16.9 %collective-permute-start.17 = (bf16[1,1808,128]{2,1,0:T(8,128)(2,1)S(1)}, bf16[1,1808,128]{2,1,0:T(8,128)(2,1)S(1)}, u32[]{:S(2)}, u32[]{:S(2)}) collective-permute-start(bf16[1,1808,128]{2,1,0:T(8,128)(2,1)S(1)} %pad_maximum_fusion.1), channel_id=1, source_target_pairs={{2,3},{6,7},{10,11},{14,15},{18,19},{22,23},{26,27},{30,31}} | collective-permute-start | bytes 1388552 | tf_op jit(solution)/shard_map/ppermute | solution.py:359
  107.4 13.9 %collective-permute-start.14 = (bf16[1536,128]{1,0:T(8,128)(2,1)S(1)}, bf16[1536,128]{1,0:T(8,128)(2,1)S(1)}, u32[]{:S(2)}, u32[]{:S(2)}) collective-permute-start(bf16[1536,128]{1,0:T(8,128)(2,1)S(1)} %slice.150), channel_id=1, source_target_pairs={{1,0},{5,4},{9,8},{13,12},{17,16},{21,20},{25,24},{29,28}} | collective-permute-start | bytes 1179656 | tf_op jit(solution)/shard_map/ppermute | solution.py:359
  111.4 19.9 %collective-permute-start.21 = (bf16[1808,128]{1,0:T(8,128)(2,1)S(1)}, bf16[1808,128]{1,0:T(8,128)(2,1)S(1)}, u32[]{:S(2)}, u32[]{:S(2)}) collective-permute-start(bf16[1808,128]{1,0:T(8,128)(2,1)S(1)} %collective-permute-done.20.left1), channel_id=1, source_target_pairs={{1,0},{2,1},{5,4},{6,5},{9,8},{10,9},{13,12},{14,13},{17,16},{18,1... | collective-permute-start | bytes 1388552 | tf_op jit(solution)/shard_map/ppermute | solution.py:359
  112.9 20.6 %collective-permute-start.2 = (s32[4,257]{1,0:T(4,128)S(1)}, s32[4,257]{1,0:T(4,128)S(1)}, u32[]{:S(2)}, u32[]{:S(2)}) collective-permute-start(s32[4,257]{1,0:T(4,128)S(1)} %get-tuple-element.24), channel_id=1, source_target_pairs={{0,8},{8,0},{4,12},{12,4},{16,24},{24,16},{20,28},{28,20},{1,9},{9... | collective-permute-start | bytes 12344 | tf_op jit(solution)/shard_map/ppermute | solution.py:423
  116.5 24.9 %collective-permute-start.28 = (bf16[1808,128]{1,0:T(8,128)(2,1)}, bf16[1808,128]{1,0:T(8,128)(2,1)}, u32[]{:S(2)}, u32[]{:S(2)}) collective-permute-start(bf16[1808,128]{1,0:T(8,128)(2,1)} %fusion.3), channel_id=1, source_target_pairs={{1,0},{2,1},{3,2},{5,4},{6,5},{7,6},{9,8},{10,9},{11,10},{13,12},{... | collective-permute-start | bytes 1388552 | tf_op jit(solution)/shard_map/ppermute | solution.py:359
  117.8 25.0 %collective-permute-start.32 = (bf16[1,1808,128]{2,1,0:T(8,128)(2,1)}, bf16[1,1808,128]{2,1,0:T(8,128)(2,1)}, u32[]{:S(2)}, u32[]{:S(2)}) collective-permute-start(bf16[1,1808,128]{2,1,0:T(8,128)(2,1)} %collective-permute-done.31.right0), channel_id=1, source_target_pairs={{1,2},{2,3},{5,6},{6,7},{9,10},{10,11},{13,14},{14,15},{17,18},{18... | collective-permute-start | bytes 1388552 | tf_op jit(solution)/shard_map/ppermute | solution.py:359
  125.4 19.8 %collective-permute-start.18 = (bf16[4,256,256]{2,1,0:T(8,128)(2,1)}, bf16[4,256,256]{2,1,0:T(8,128)(2,1)}, u32[]{:S(2)}, u32[]{:S(2)}) collective-permute-start(bf16[4,256,256]{2,1,0:T(8,128)(2,1)} %get-tuple-element.32.own_ref), channel_id=1, source_target_pairs={{0,8},{8,0},{4,12},{12,4},{16,24},{24,16},{20,28},{28,20},{1,9},{9... | collective-permute-start | bytes 1572872 | tf_op jit(solution)/shard_map/ppermute | solution.py:443
  131.3 19.3 %collective-permute-start.25 = (bf16[1,1808,128]{2,1,0:T(8,128)(2,1)}, bf16[1,1808,128]{2,1,0:T(8,128)(2,1)}, u32[]{:S(2)}, u32[]{:S(2)}) collective-permute-start(bf16[1,1808,128]{2,1,0:T(8,128)(2,1)} %pad_maximum_fusion.2), channel_id=1, source_target_pairs={{2,3},{6,7},{10,11},{14,15},{18,19},{22,23},{26,27},{30,31}} | collective-permute-start | bytes 1388552 | tf_op jit(solution)/shard_map/ppermute | solution.py:359
  133.5 17.1 %collective-permute-start.22 = (bf16[1536,128]{1,0:T(8,128)(2,1)}, bf16[1536,128]{1,0:T(8,128)(2,1)}, u32[]{:S(2)}, u32[]{:S(2)}) collective-permute-start(bf16[1536,128]{1,0:T(8,128)(2,1)} %slice.154), channel_id=1, source_target_pairs={{1,0},{5,4},{9,8},{13,12},{17,16},{21,20},{25,24},{29,28}} | collective-permute-start | bytes 1179656 | tf_op jit(solution)/shard_map/ppermute | solution.py:359
  141.3 16.8 %collective-permute-start.29 = (bf16[1808,128]{1,0:T(8,128)(2,1)}, bf16[1808,128]{1,0:T(8,128)(2,1)S(1)}, u32[]{:S(2)}, u32[]{:S(2)}) collective-permute-start(bf16[1808,128]{1,0:T(8,128)(2,1)} %collective-permute-done.28.left1), channel_id=1, source_target_pairs={{1,0},{2,1},{5,4},{6,5},{9,8},{10,9},{13,12},{14,13},{17,16},{18,1... | collective-permute-start | bytes 1388552 | tf_op jit(solution)/shard_map/ppermute | solution.py:359
  142.8 16.9 %collective-permute-start.1 = (s32[4,257]{1,0:T(4,128)S(1)}, s32[4,257]{1,0:T(4,128)S(1)}, u32[]{:S(2)}, u32[]{:S(2)}) collective-permute-start(s32[4,257]{1,0:T(4,128)S(1)} %get-tuple-element.23), channel_id=1, source_target_pairs={{0,16},{16,0},{4,20},{20,4},{8,24},{24,8},{12,28},{28,12},{1,17},{... | collective-permute-start | bytes 12344 | tf_op jit(solution)/shard_map/ppermute | solution.py:423
  157.4 12.4 %collective-permute-start.33 = (bf16[1,1808,128]{2,1,0:T(8,128)(2,1)}, bf16[1,1808,128]{2,1,0:T(8,128)(2,1)S(1)}, u32[]{:S(2)}, u32[]{:S(2)}) collective-permute-start(bf16[1,1808,128]{2,1,0:T(8,128)(2,1)} %pad_maximum_fusion.3), channel_id=1, source_target_pairs={{2,3},{6,7},{10,11},{14,15},{18,19},{22,23},{26,27},{30,31}} | collective-permute-start | bytes 1388552 | tf_op jit(solution)/shard_map/ppermute | solution.py:359
  158.1 11.6 %collective-permute-start.30 = (bf16[1536,128]{1,0:T(8,128)(2,1)S(1)}, bf16[1536,128]{1,0:T(8,128)(2,1)S(1)}, u32[]{:S(2)}, u32[]{:S(2)}) collective-permute-start(bf16[1536,128]{1,0:T(8,128)(2,1)S(1)} %slice.158), channel_id=1, source_target_pairs={{1,0},{5,4},{9,8},{13,12},{17,16},{21,20},{25,24},{29,28}} | collective-permute-start | bytes 1179656 | tf_op jit(solution)/shard_map/ppermute | solution.py:359
  (27 other events, 423.7 us)

commit v3 on v1

--- a/solution.py
+++ b/solution.py
@@ -7,6 +7,10 @@
 from jax.experimental.pallas import tpu as pltpu
 from jax.sharding import PartitionSpec as P
 
+TIE = 0
+TIE_TO = (1,)
+TABLE_TIE = True
+RIGHT_GROUPS = [[0], [1], [2], [3]]
 LANES = 128
 SPARE = 16
 ANY = pl.BlockSpec(memory_space=pl.ANY)
@@ -349,22 +353,28 @@
     place_ref = place[None]
     up = [(0, 1), (1, 2), (2, 3)]
     down = [(1, 0), (2, 1), (3, 2)]
-    packs = [pack(place_ref, diag_inv, below_panel, t) for t in range(tiers)]
-
-    lefts = []
-    for base, rest in packs:
+    packs = []
+    for t in range(tiers):
+        panels = below_panel
+        if t > 0:
+            panels = lax.optimization_barrier((below_panel, packs[t - 1][0]))[0]
+        packs.append(pack(place_ref, diag_inv, panels, t))
+
+    lefts, rights = [], []
+    for t, (base, rest) in enumerate(packs):
+        if TIE and t >= TIE:
+            base = after(base, *[lefts[t - TIE][i] for i in TIE_TO])
         left0 = send(base, down)
         mixed = jnp.concatenate([rest[block : 2 * block], left0[block:]], 0)
         left1 = send(jnp.where(place == 1, left0, jnp.where(place == 2, mixed, rest)), down)
         left2 = send(left1, down[:2])
-        left3 = send(left2[: 3 * block], down[:1])
+        straight = t == tiers - 1
+        left3 = send(rest[: 3 * block], [(3, 0)]) if straight else send(left2[: 3 * block], down[:1])
         lefts.append((left0, left1, left2, left3))
-
-    rights = []
-    for group in right_groups(tiers):
+    for group in RIGHT_GROUPS:
         bases = jnp.stack([packs[t][0] for t in group])
         if group[0] > 0:
-            bases = after(bases, lefts[0][1])
+            bases = after(bases, lefts[group[0] - 1][1])
         right0 = send(bases, up)
         right1 = send(right0, up[1:])
         second = jnp.stack([packs[t][1][block : 2 * block] for t in group])
@@ -375,7 +385,10 @@
     count = lax.axis_size("leaf")
     bit_count = max(count.bit_length() - 1, 1)
     table = jnp.concatenate([parent_map[:, :, None], row_lists], 2)
-    tables = lax.all_gather(table, "leaf")
+    tables = []
+    for t in range(tiers - 1):
+        mine = after(table[t], lefts[0][0]) if TABLE_TIE else table[t]
+        tables.append(lax.ppermute(mine, "leaf", swap_route("leaf", t % bit_count)))
     source, first_block = histograms.reshape(-1, columns, width), 0
     solved = None
     for t in range(tiers):
@@ -397,7 +410,7 @@
         bit = t % bit_count
         peer = lax.ppermute(update, "leaf", swap_route("leaf", bit))
         partner = jnp.bitwise_xor(myself, 1 << bit)
-        theirs = lax.dynamic_index_in_dim(tables, jnp.minimum(partner, count - 1), 0, False)[t]
+        theirs = tables[t]
         parents = jnp.concatenate([parent_map[t], theirs[:, 0]])
         exists = jnp.repeat(jnp.stack([partner >= 0, partner < count]), per_device)
         mine = jnp.logical_and(parents // per_device == myself, exists)
@@ -405,10 +418,6 @@
         source = source_of(histograms, t + 1, update, peer, slots, row_lists[t], theirs[:, 1:])
         first_block = 0
     return solved, update
-
-
-def right_groups(tiers):
-    return [[0], list(range(1, tiers))]
 
 
 def on_device(histograms, diag_inv, below_panel, parent_map, row_lists):

time: 208 us -> 177 us (0.85); the launches traced: 205 us -> 176 us
  waiting for transfers between devices: 95.3 us -> 62.2 us
  starting transfers between devices: 37.1 us -> 53.7 us
  blocking collectives: 9.25 us -> 0 us
  Pallas kernels: 32.3 us -> 29.2 us
    ppermute x22 -> x28, waiting for transfers between devices: 88.6 us -> 45.8 us  [send(): return lax.ppermute(value, 'col', route)]
    ppermute x22 -> x28, starting transfers between devices: 33.9 us -> 48.3 us  [send(): return lax.ppermute(value, 'col', route)]
    ppermute x3, waiting for transfers between devices: 6.76 us -> 16.4 us  [line_plan(): peer = lax.ppermute(update, 'leaf', swap_route('leaf', bit))]
    all_gather x1 -> x0, blocking collectives: 9.25 us -> none  [line_plan(): tables = lax.all_gather(table, 'leaf')]
    slice x6 -> x4, local copies, waits for them, and re-layouts: 6.7 us -> 2.62 us  [the longest x3 1.84 us: line_plan(): left2[:3 * block]]
    another operation x2 -> x4, local copies, waits for them, and re-layouts: 3.26 us -> 5.88 us  [line_plan(): second = jnp.stack([packs[t][1][block:2 * block] for t in group])]
    another operation x1 -> x0, other arithmetic: 2.53 us -> none  [line_plan(): bases = jnp.stack([packs[t][0] for t in group])]
    pallas_call x3, Pallas kernels: 7.25 us -> 4.74 us  [source_of(): pl.pallas_call(source_kernel, grid=(1,), in_specs=[SMEM, pl.BlockSpec((1,...]
  transfers between devices with their start and end apart: 25 -> 34, of which waited for: 12 -> 8; matrix products, arithmetic and copies ran while one was open for 9% -> 11% of each run, Pallas kernels for 10% -> 13%
where the time goes in v3:
time: 177 us; the launch traced here: 176 us
  waiting for transfers between devices  62.2 us (35%)
  starting transfers between devices  53.7 us (30%)
  Pallas kernels  29.2 us (16%)
  local copies, waits for them, and re-layouts  22.4 us (13%)
  other arithmetic  6.75 us (4%)
    ppermute x28, starting transfers between devices, send(): return lax.ppermute(value, 'col', route)  48.3 us
    ppermute x28, waiting for transfers between devices, send(): return lax.ppermute(value, 'col', route)  45.8 us
    ppermute x3, waiting for transfers between devices, line_plan(): peer = lax.ppermute(update, 'leaf', swap_route('leaf', bit))  16.4 us
    pallas_call x4, Pallas kernels, solve(): pl.pallas_call(functools.partial(solve_kernel, group_at, has_prior), grid...  15.3 us
    unnamed x60, local copies, waits for them, and re-layouts  10.6 us
    pallas_call x4, Pallas kernels, pack(): pl.pallas_call(pack_kernel, grid=(1,), in_specs=[SMEM, pl.BlockSpec((1, p...  9.23 us
    another operation x4, local copies, waits for them, and re-layouts, line_plan(): second = jnp.stack([packs[t][1][block:2 * block] for t in group])  5.88 us
    pallas_call x3, Pallas kernels, source_of(): pl.pallas_call(source_kernel, grid=(1,), in_specs=[SMEM, pl.BlockSpec((1,...  4.74 us
  transfers between devices with their start and end apart: 34, of which 8 were waited for; matrix products, arithmetic and copies ran while one was open for 11% of the time, Pallas kernels for 13%

profile of v3, /device:TPU:0, one launch (start us, length us, event | category | flops | bytes accessed | tf_op | source)
XLA Modules:
  0.0 175.8 jit_solution(6477591721311889814)
XLA Ops:
  0.7 2.3 %pack_0.1 = (bf16[1808,128]{1,0:T(8,128)(2,1)}, bf16[1808,128]{1,0:T(8,128)(2,1)}) custom-call(s32[1]{0:T(128)} %bitcast.place_ref, bf16[4,4,128,512]{3,2,1,0:T(8,128)(2,1)} %diag_ref.7, bf16[4,4,64,512]{3,2,1,0:T(8,128)(2,1)} %below_ref.4), custom_call_target="tpu_custom_call" | custom-call | bytes 1851392 | tf_op jit(solution)/shard_map/pack_0/pallas_call | solution.py:130
  4.2 6.3 %collective-permute-start.7 = (bf16[1,1808,128]{2,1,0:T(8,128)(2,1)}, bf16[1,1808,128]{2,1,0:T(8,128)(2,1)}, u32[]{:S(2)}, u32[]{:S(2)}) collective-permute-start(bf16[1,1808,128]{2,1,0:T(8,128)(2,1)} %bitcast.42), channel_id=1, source_target_pairs={{0,1},{1,2},{2,3},{4,5},{5,6},{6,7},{8,9},{9,10},{10,11},{12,13},{... | collective-permute-start | bytes 1388552 | tf_op jit(solution)/shard_map/ppermute | solution.py:345
  10.6 2.3 %pack_1.1 = (bf16[1808,128]{1,0:T(8,128)(2,1)}, bf16[1808,128]{1,0:T(8,128)(2,1)}) custom-call(s32[1]{0:T(128)} %bitcast.place_ref, bf16[4,4,128,512]{3,2,1,0:T(8,128)(2,1)} %diag_ref.7, bf16[4,4,64,512]{3,2,1,0:T(8,128)(2,1)} %below_ref.4), custom_call_target="tpu_custom_call" | custom-call | bytes 1851392 | tf_op jit(solution)/shard_map/pack_1/pallas_call | solution.py:130
  14.1 5.3 %collective-permute-start.15 = (bf16[1,1808,128]{2,1,0:T(8,128)(2,1)}, bf16[1,1808,128]{2,1,0:T(8,128)(2,1)}, u32[]{:S(2)}, u32[]{:S(2)}) collective-permute-start(bf16[1,1808,128]{2,1,0:T(8,128)(2,1)} %bitcast.41), channel_id=1, source_target_pairs={{0,1},{1,2},{2,3},{4,5},{5,6},{6,7},{8,9},{9,10},{10,11},{12,13},{... | collective-permute-start | bytes 1388552 | tf_op jit(solution)/shard_map/ppermute | solution.py:345
  19.5 2.3 %pack_2.1 = (bf16[1808,128]{1,0:T(8,128)(2,1)}, bf16[1808,128]{1,0:T(8,128)(2,1)}) custom-call(s32[1]{0:T(128)} %bitcast.place_ref, bf16[4,4,128,512]{3,2,1,0:T(8,128)(2,1)} %diag_ref.7, bf16[4,4,64,512]{3,2,1,0:T(8,128)(2,1)} %below_ref.4), custom_call_target="tpu_custom_call" | custom-call | bytes 1851392 | tf_op jit(solution)/shard_map/pack_2/pallas_call | solution.py:130
  23.2 1.7 slice_bitcast_fusion.9
  24.8 1.6 slice_bitcast_fusion.8
  26.5 2.3 %pack_3.1 = (bf16[1808,128]{1,0:T(8,128)(2,1)}, bf16[1808,128]{1,0:T(8,128)(2,1)}) custom-call(s32[1]{0:T(128)} %bitcast.place_ref, bf16[4,4,128,512]{3,2,1,0:T(8,128)(2,1)} %diag_ref.7, bf16[4,4,64,512]{3,2,1,0:T(8,128)(2,1)} %below_ref.4), custom_call_target="tpu_custom_call" | custom-call | bytes 1851392 | tf_op jit(solution)/shard_map/pack_3/pallas_call | solution.py:130
  29.8 1.7 slice_bitcast_fusion.6
  31.5 4.7 %collective-permute-start.23 = (bf16[1,1808,128]{2,1,0:T(8,128)(2,1)}, bf16[1,1808,128]{2,1,0:T(8,128)(2,1)S(1)}, u32[]{:S(2)}, u32[]{:S(2)}) collective-permute-start(bf16[1,1808,128]{2,1,0:T(8,128)(2,1)} %bitcast.21), channel_id=1, source_target_pairs={{0,1},{1,2},{2,3},{4,5},{5,6},{6,7},{8,9},{9,10},{10,11},{12,13},{... | collective-permute-start | bytes 1388552 | tf_op jit(solution)/shard_map/ppermute | solution.py:345
  40.9 2.0 %fusion.1 = bf16[1808,128]{1,0:T(8,128)(2,1)} fusion(bf16[1808,128]{1,0:T(8,128)(2,1)S(1)} %collective-permute-done.11.left0, bf16[1808,128]{1,0:T(8,128)(2,1)} %get-tuple-element.30.rest, bf16[1296,128]{1,0:T(8,128)(2,1)S(1)} %slice.149, bf16[512,128]{1,0:T(8,128)(2,1)S(1)} %copy-done.27, pred[]{:T(512)S(6)} %eq.35, pred[]{:T(512)S(6)} %eq.34), kind=kLoop, calls=%fused_computation.4 | loop fusion | flops 1388544 | bytes 1851394 | tf_op jit(solution)/shard_map/jit(_where)/select_n | solution.py:369
  42.9 16.3 %collective-permute-done.4.left1 = bf16[1808,128]{1,0:T(8,128)(2,1)S(1)} collective-permute-done((bf16[1808,128]{1,0:T(8,128)(2,1)S(1)}, bf16[1808,128]{1,0:T(8,128)(2,1)S(1)}, u32[]{:S(2)}, u32[]{:S(2)}) %collective-permute-start.4) | collective-permute-done | bytes 462880 | tf_op jit(solution)/shard_map/ppermute | solution.py:345
  62.9 11.6 %collective-permute-done.5.left2 = bf16[1808,128]{1,0:T(8,128)(2,1)S(1)} collective-permute-done((bf16[1808,128]{1,0:T(8,128)(2,1)S(1)}, bf16[1808,128]{1,0:T(8,128)(2,1)S(1)}, u32[]{:S(2)}, u32[]{:S(2)}) %collective-permute-start.5) | collective-permute-done | bytes 462880 | tf_op jit(solution)/shard_map/ppermute | solution.py:345
  74.5 1.5 collective-permute-start.16
  78.9 1.5 collective-permute-start.9
  81.8 1.4 collective-permute-start.24
  88.1 6.3 %collective-permute-done.20.left1 = bf16[1808,128]{1,0:T(8,128)(2,1)} collective-permute-done((bf16[1808,128]{1,0:T(8,128)(2,1)}, bf16[1808,128]{1,0:T(8,128)(2,1)}, u32[]{:S(2)}, u32[]{:S(2)}) %collective-permute-start.20) | collective-permute-done | bytes 462880 | tf_op jit(solution)/shard_map/ppermute | solution.py:345
  94.4 2.8 %collective-permute-start.31 = (bf16[1,1808,128]{2,1,0:T(8,128)(2,1)}, bf16[1,1808,128]{2,1,0:T(8,128)(2,1)S(1)}, u32[]{:S(2)}, u32[]{:S(2)}) collective-permute-start(bf16[1,1808,128]{2,1,0:T(8,128)(2,1)} %bitcast.40), channel_id=1, source_target_pairs={{0,1},{1,2},{2,3},{4,5},{5,6},{6,7},{8,9},{9,10},{10,11},{12,13},{... | collective-permute-start | bytes 1388552 | tf_op jit(solution)/shard_map/ppermute | solution.py:345
  98.5 4.2 %collective-permute-done.6.left3 = bf16[1536,128]{1,0:T(8,128)(2,1)S(1)} collective-permute-done((bf16[1536,128]{1,0:T(8,128)(2,1)}, bf16[1536,128]{1,0:T(8,128)(2,1)S(1)}, u32[]{:S(2)}, u32[]{:S(2)}) %collective-permute-start.6) | collective-permute-done | bytes 393248 | tf_op jit(solution)/shard_map/ppermute | solution.py:345
  102.7 2.2 %copy-done = bf16[4,4,256,512]{3,2,1,0:T(8,128)(2,1)S(1)} copy-done((bf16[4,4,256,512]{3,2,1,0:T(8,128)(2,1)S(1)}, bf16[4,4,256,512]{3,2,1,0:T(8,128)(2,1)}, u32[]{:S(2)}) %copy-start) | copy-done | bytes 4194328
  110.0 3.6 %solve_0.1 = (bf16[4,4,256,512]{3,2,1,0:T(8,128)(2,1)}, bf16[4,256,256]{2,1,0:T(8,128)(2,1)S(1)}) custom-call(s32[1]{0:T(128)} %bitcast.place_ref, bf16[16,256,512]{2,1,0:T(8,128)(2,1)S(1)} %bitcast.39, bf16[1808,128]{1,0:T(8,128)(2,1)S(1)} %copy-done.21, bf16[1808,128]{1,0:T(8,128)(2,1)S(1)} %copy-done.8, bf16[1808,128]{1,0:T(8,128)(2,1)S(1)} %collective-permute-done.left0, ...), custom_call_target="tpu_custom_call" | custom-call | flops 805306368 | bytes 3145728 | tf_op jit(solution)/shard_map/solve_0/pallas_call | solution.py:309
  122.9 6.0 %collective-permute-done.14.left3 = bf16[1536,128]{1,0:T(8,128)(2,1)S(1)} collective-permute-done((bf16[1536,128]{1,0:T(8,128)(2,1)S(1)}, bf16[1536,128]{1,0:T(8,128)(2,1)S(1)}, u32[]{:S(2)}, u32[]{:S(2)}) %collective-permute-start.14) | collective-permute-done | bytes 393248 | tf_op jit(solution)/shard_map/ppermute | solution.py:345
  128.9 3.9 %solve_1.1 = (bf16[4,4,256,512]{3,2,1,0:T(8,128)(2,1)}, bf16[4,256,256]{2,1,0:T(8,128)(2,1)S(1)}) custom-call(s32[1]{0:T(128)} %bitcast.place_ref, bf16[4,256,512]{2,1,0:T(8,128)(2,1)S(1)} %source_1.1.source_ref, bf16[1808,128]{1,0:T(8,128)(2,1)S(1)} %copy-done.18, bf16[1808,128]{1,0:T(8,128)(2,1)S(1)} %copy-done.7, ...), custom_call_target="tpu_custom_call", output_to_operand_aliasing={{0}: (11, {})} | custom-call | flops 805306368 | bytes 3145728 | tf_op jit(solution)/shard_map/solve_1/pallas_call | solution.py:309
  132.8 1.6 collective-permute-start.18
  137.5 8.9 %collective-permute-done.18.peer_ref = bf16[4,256,256]{2,1,0:T(8,128)(2,1)S(1)} collective-permute-done((bf16[4,256,256]{2,1,0:T(8,128)(2,1)S(1)}, bf16[4,256,256]{2,1,0:T(8,128)(2,1)S(1)}, u32[]{:S(2)}, u32[]{:S(2)}) %collective-permute-start.18) | collective-permute-done | bytes 524320 | tf_op jit(solution)/shard_map/ppermute | solution.py:411
  147.5 2.6 %source_2.1.source_ref = bf16[4,256,512]{2,1,0:T(8,128)(2,1)S(1)} custom-call(s32[8]{0:T(128)S(1)} %and_select_fusion.4.slots_ref, bf16[4,4,256,512]{3,2,1,0:T(8,128)(2,1)S(1)} %copy-done.1, bf16[4,256,256]{2,1,0:T(8,128)(2,1)S(1)} %get-tuple-element.32.own_ref, bf16[4,256,256]{2,1,0:T(8,128)(2,1)S(1)} %collective-permute-done.18.peer_ref, ...), custom_call_target="tpu_custom_call" | custom-call | flops 536870912 | bytes 3145728 | tf_op jit(solution)/shard_map/source_2/pallas_call | solution.py:171
  150.1 3.8 %solve_2.1 = (bf16[4,4,256,512]{3,2,1,0:T(8,128)(2,1)}, bf16[4,256,256]{2,1,0:T(8,128)(2,1)S(1)}) custom-call(s32[1]{0:T(128)} %bitcast.place_ref, bf16[4,256,512]{2,1,0:T(8,128)(2,1)S(1)} %source_2.1.source_ref, bf16[1808,128]{1,0:T(8,128)(2,1)} %get-tuple-element.34.base, bf16[1808,128]{1,0:T(8,128)(2,1)S(1)} %copy-done.6, ...), custom_call_target="tpu_custom_call", output_to_operand_aliasing={{0}: (11, {})} | custom-call | flops 805306368 | bytes 3145728 | tf_op jit(solution)/shard_map/solve_2/pallas_call | solution.py:309
  154.0 1.5 collective-permute-start.26
  156.3 1.4 collective-permute-start.33
  159.5 7.5 %collective-permute-done.26.peer_ref = bf16[4,256,256]{2,1,0:T(8,128)(2,1)S(1)} collective-permute-done((bf16[4,256,256]{2,1,0:T(8,128)(2,1)S(1)}, bf16[4,256,256]{2,1,0:T(8,128)(2,1)S(1)}, u32[]{:S(2)}, u32[]{:S(2)}) %collective-permute-start.26) | collective-permute-done | bytes 524320 | tf_op jit(solution)/shard_map/ppermute | solution.py:411
  167.0 2.2 %copy-done.2 = bf16[4,4,256,512]{3,2,1,0:T(8,128)(2,1)S(1)} copy-done((bf16[4,4,256,512]{3,2,1,0:T(8,128)(2,1)S(1)}, bf16[4,4,256,512]{3,2,1,0:T(8,128)(2,1)}, u32[]{:S(2)}) %copy-start.2) | copy-done | bytes 4194328
  171.6 4.0 %solve_3.1 = (bf16[4,4,256,512]{3,2,1,0:T(8,128)(2,1)}, bf16[4,256,256]{2,1,0:T(8,128)(2,1)}) custom-call(s32[1]{0:T(128)} %bitcast.place_ref, bf16[4,256,512]{2,1,0:T(8,128)(2,1)S(1)} %source_3.1.source_ref, bf16[1808,128]{1,0:T(8,128)(2,1)S(1)} %copy-done.15, bf16[1808,128]{1,0:T(8,128)(2,1)S(1)} %copy-done.3, ...), custom_call_target="tpu_custom_call", output_to_operand_aliasing={{0}: (11, {})} | custom-call | flops 805306368 | bytes 3145728 | tf_op jit(solution)/shard_map/solve_3/pallas_call | solution.py:309
  (154 shorter events, 47.1 us)
Async XLA Ops:
  2.9 28.5 %collective-permute-start = (bf16[1808,128]{1,0:T(8,128)(2,1)}, bf16[1808,128]{1,0:T(8,128)(2,1)S(1)}, u32[]{:S(2)}, u32[]{:S(2)}) collective-permute-start(bf16[1808,128]{1,0:T(8,128)(2,1)} %get-tuple-element.22.base), channel_id=1, source_target_pairs={{1,0},{2,1},{3,2},{5,4},{6,5},{7,6},{9,8},{10,9},{11,10},{13,12},{... | collective-permute-start | bytes 1388552 | tf_op jit(solution)/shard_map/ppermute | solution.py:345
  4.2 34.6 %collective-permute-start.7 = (bf16[1,1808,128]{2,1,0:T(8,128)(2,1)}, bf16[1,1808,128]{2,1,0:T(8,128)(2,1)}, u32[]{:S(2)}, u32[]{:S(2)}) collective-permute-start(bf16[1,1808,128]{2,1,0:T(8,128)(2,1)} %bitcast.42), channel_id=1, source_target_pairs={{0,1},{1,2},{2,3},{4,5},{5,6},{6,7},{8,9},{9,10},{10,11},{12,13},{... | collective-permute-start | bytes 1388552 | tf_op jit(solution)/shard_map/ppermute | solution.py:345
  12.8 23.4 %collective-permute-start.11 = (bf16[1808,128]{1,0:T(8,128)(2,1)}, bf16[1808,128]{1,0:T(8,128)(2,1)S(1)}, u32[]{:S(2)}, u32[]{:S(2)}) collective-permute-start(bf16[1808,128]{1,0:T(8,128)(2,1)} %get-tuple-element.29.base), channel_id=1, source_target_pairs={{1,0},{2,1},{3,2},{5,4},{6,5},{7,6},{9,8},{10,9},{11,10},{13,12},{... | collective-permute-start | bytes 1388552 | tf_op jit(solution)/shard_map/ppermute | solution.py:345
  14.1 47.4 %collective-permute-start.15 = (bf16[1,1808,128]{2,1,0:T(8,128)(2,1)}, bf16[1,1808,128]{2,1,0:T(8,128)(2,1)}, u32[]{:S(2)}, u32[]{:S(2)}) collective-permute-start(bf16[1,1808,128]{2,1,0:T(8,128)(2,1)} %bitcast.41), channel_id=1, source_target_pairs={{0,1},{1,2},{2,3},{4,5},{5,6},{6,7},{8,9},{9,10},{10,11},{12,13},{... | collective-permute-start | bytes 1388552 | tf_op jit(solution)/shard_map/ppermute | solution.py:345
  21.8 18.4 %collective-permute-start.19 = (bf16[1808,128]{1,0:T(8,128)(2,1)}, bf16[1808,128]{1,0:T(8,128)(2,1)S(1)}, u32[]{:S(2)}, u32[]{:S(2)}) collective-permute-start(bf16[1808,128]{1,0:T(8,128)(2,1)} %get-tuple-element.34.base), channel_id=1, source_target_pairs={{1,0},{2,1},{3,2},{5,4},{6,5},{7,6},{9,8},{10,9},{11,10},{13,12},{... | collective-permute-start | bytes 1388552 | tf_op jit(solution)/shard_map/ppermute | solution.py:345
  31.5 46.1 %collective-permute-start.23 = (bf16[1,1808,128]{2,1,0:T(8,128)(2,1)}, bf16[1,1808,128]{2,1,0:T(8,128)(2,1)S(1)}, u32[]{:S(2)}, u32[]{:S(2)}) collective-permute-start(bf16[1,1808,128]{2,1,0:T(8,128)(2,1)} %bitcast.21), channel_id=1, source_target_pairs={{0,1},{1,2},{2,3},{4,5},{5,6},{6,7},{8,9},{9,10},{10,11},{12,13},{... | collective-permute-start | bytes 1388552 | tf_op jit(solution)/shard_map/ppermute | solution.py:345
  36.2 42.6 %collective-permute-start.27 = (bf16[1808,128]{1,0:T(8,128)(2,1)}, bf16[1808,128]{1,0:T(8,128)(2,1)S(1)}, u32[]{:S(2)}, u32[]{:S(2)}) collective-permute-start(bf16[1808,128]{1,0:T(8,128)(2,1)} %get-tuple-element.39.base), channel_id=1, source_target_pairs={{1,0},{2,1},{3,2},{5,4},{6,5},{7,6},{9,8},{10,9},{11,10},{13,12},{... | collective-permute-start | bytes 1388552 | tf_op jit(solution)/shard_map/ppermute | solution.py:345
  38.9 20.3 %collective-permute-start.4 = (bf16[1808,128]{1,0:T(8,128)(2,1)S(1)}, bf16[1808,128]{1,0:T(8,128)(2,1)S(1)}, u32[]{:S(2)}, u32[]{:S(2)}) collective-permute-start(bf16[1808,128]{1,0:T(8,128)(2,1)S(1)} %fusion), channel_id=1, source_target_pairs={{1,0},{2,1},{3,2},{5,4},{6,5},{7,6},{9,8},{10,9},{11,10},{13,12},{... | collective-permute-start | bytes 1388552 | tf_op jit(solution)/shard_map/ppermute | solution.py:345
  40.2 21.3 %collective-permute-start.8 = (bf16[1,1808,128]{2,1,0:T(8,128)(2,1)}, bf16[1,1808,128]{2,1,0:T(8,128)(2,1)S(1)}, u32[]{:S(2)}, u32[]{:S(2)}) collective-permute-start(bf16[1,1808,128]{2,1,0:T(8,128)(2,1)} %collective-permute-done.7.right0), channel_id=1, source_target_pairs={{1,2},{2,3},{5,6},{6,7},{9,10},{10,11},{13,14},{14,15},{17,18},{18... | collective-permute-start | bytes 1388552 | tf_op jit(solution)/shard_map/ppermute | solution.py:345
  59.2 15.3 %collective-permute-start.5 = (bf16[1808,128]{1,0:T(8,128)(2,1)S(1)}, bf16[1808,128]{1,0:T(8,128)(2,1)S(1)}, u32[]{:S(2)}, u32[]{:S(2)}) collective-permute-start(bf16[1808,128]{1,0:T(8,128)(2,1)S(1)} %collective-permute-done.4.left1), channel_id=1, source_target_pairs={{1,0},{2,1},{5,4},{6,5},{9,8},{10,9},{13,12},{14,13},{17,16},{18,1... | collective-permute-start | bytes 1388552 | tf_op jit(solution)/shard_map/ppermute | solution.py:345
  61.5 18.8 %collective-permute-start.3 = (s32[4,257]{1,0:T(4,128)S(1)}, s32[4,257]{1,0:T(4,128)S(1)}, u32[]{:S(2)}, u32[]{:S(2)}) collective-permute-start(s32[4,257]{1,0:T(4,128)S(1)} %get-tuple-element.25), channel_id=1, source_target_pairs={{0,4},{4,0},{8,12},{12,8},{16,20},{20,16},{24,28},{28,24},{1,5},{5... | collective-permute-start | bytes 12344 | tf_op jit(solution)/shard_map/ppermute | solution.py:391
  61.6 22.9 %collective-permute-start.12 = (bf16[1808,128]{1,0:T(8,128)(2,1)}, bf16[1808,128]{1,0:T(8,128)(2,1)}, u32[]{:S(2)}, u32[]{:S(2)}) collective-permute-start(bf16[1808,128]{1,0:T(8,128)(2,1)} %fusion.1), channel_id=1, source_target_pairs={{1,0},{2,1},{3,2},{5,4},{6,5},{7,6},{9,8},{10,9},{11,10},{13,12},{... | collective-permute-start | bytes 1388552 | tf_op jit(solution)/shard_map/ppermute | solution.py:345
  77.6 16.9 %collective-permute-start.20 = (bf16[1808,128]{1,0:T(8,128)(2,1)}, bf16[1808,128]{1,0:T(8,128)(2,1)}, u32[]{:S(2)}, u32[]{:S(2)}) collective-permute-start(bf16[1808,128]{1,0:T(8,128)(2,1)} %fusion.2), channel_id=1, source_target_pairs={{1,0},{2,1},{3,2},{5,4},{6,5},{7,6},{9,8},{10,9},{11,10},{13,12},{... | collective-permute-start | bytes 1388552 | tf_op jit(solution)/shard_map/ppermute | solution.py:345
  78.9 18.4 %collective-permute-start.9 = (bf16[1,1808,128]{2,1,0:T(8,128)(2,1)}, bf16[1,1808,128]{2,1,0:T(8,128)(2,1)}, u32[]{:S(2)}, u32[]{:S(2)}) collective-permute-start(bf16[1,1808,128]{2,1,0:T(8,128)(2,1)} %pad_maximum_fusion), channel_id=1, source_target_pairs={{2,3},{6,7},{10,11},{14,15},{18,19},{22,23},{26,27},{30,31}} | collective-permute-start | bytes 1388552 | tf_op jit(solution)/shard_map/ppermute | solution.py:345
  80.4 22.4 %collective-permute-start.6 = (bf16[1536,128]{1,0:T(8,128)(2,1)}, bf16[1536,128]{1,0:T(8,128)(2,1)S(1)}, u32[]{:S(2)}, u32[]{:S(2)}) collective-permute-start(bf16[1536,128]{1,0:T(8,128)(2,1)} %slice.146), channel_id=1, source_target_pairs={{1,0},{5,4},{9,8},{13,12},{17,16},{21,20},{25,24},{29,28}} | collective-permute-start | bytes 1179656 | tf_op jit(solution)/shard_map/ppermute | solution.py:345
  81.8 33.7 %collective-permute-start.24 = (bf16[1,1808,128]{2,1,0:T(8,128)(2,1)}, bf16[1,1808,128]{2,1,0:T(8,128)(2,1)}, u32[]{:S(2)}, u32[]{:S(2)}) collective-permute-start(bf16[1,1808,128]{2,1,0:T(8,128)(2,1)} %copy-done.16), channel_id=1, source_target_pairs={{1,2},{2,3},{5,6},{6,7},{9,10},{10,11},{13,14},{14,15},{17,18},{18... | collective-permute-start | bytes 1388552 | tf_op jit(solution)/shard_map/ppermute | solution.py:345
  84.5 29.2 %collective-permute-start.13 = (bf16[1808,128]{1,0:T(8,128)(2,1)}, bf16[1808,128]{1,0:T(8,128)(2,1)}, u32[]{:S(2)}, u32[]{:S(2)}) collective-permute-start(bf16[1808,128]{1,0:T(8,128)(2,1)} %collective-permute-done.12.left1), channel_id=1, source_target_pairs={{1,0},{2,1},{5,4},{6,5},{9,8},{10,9},{13,12},{14,13},{17,16},{18,1... | collective-permute-start | bytes 1388552 | tf_op jit(solution)/shard_map/ppermute | solution.py:345
  94.4 23.7 %collective-permute-start.31 = (bf16[1,1808,128]{2,1,0:T(8,128)(2,1)}, bf16[1,1808,128]{2,1,0:T(8,128)(2,1)S(1)}, u32[]{:S(2)}, u32[]{:S(2)}) collective-permute-start(bf16[1,1808,128]{2,1,0:T(8,128)(2,1)} %bitcast.40), channel_id=1, source_target_pairs={{0,1},{1,2},{2,3},{4,5},{5,6},{6,7},{8,9},{9,10},{10,11},{12,13},{... | collective-permute-start | bytes 1388552 | tf_op jit(solution)/shard_map/ppermute | solution.py:345
  97.2 22.0 %collective-permute-start.21 = (bf16[1808,128]{1,0:T(8,128)(2,1)}, bf16[1808,128]{1,0:T(8,128)(2,1)S(1)}, u32[]{:S(2)}, u32[]{:S(2)}) collective-permute-start(bf16[1808,128]{1,0:T(8,128)(2,1)} %collective-permute-done.20.left1), channel_id=1, source_target_pairs={{1,0},{2,1},{5,4},{6,5},{9,8},{10,9},{13,12},{14,13},{17,16},{18,1... | collective-permute-start | bytes 1388552 | tf_op jit(solution)/shard_map/ppermute | solution.py:345
  113.7 7.8 %collective-permute-start.17 = (bf16[1,1808,128]{2,1,0:T(8,128)(2,1)S(1)}, bf16[1,1808,128]{2,1,0:T(8,128)(2,1)S(1)}, u32[]{:S(2)}, u32[]{:S(2)}) collective-permute-start(bf16[1,1808,128]{2,1,0:T(8,128)(2,1)S(1)} %pad_maximum_fusion.1), channel_id=1, source_target_pairs={{2,3},{6,7},{10,11},{14,15},{18,19},{22,23},{26,27},{30,31}} | collective-permute-start | bytes 1388552 | tf_op jit(solution)/shard_map/ppermute | solution.py:345
  115.5 13.4 %collective-permute-start.14 = (bf16[1536,128]{1,0:T(8,128)(2,1)S(1)}, bf16[1536,128]{1,0:T(8,128)(2,1)S(1)}, u32[]{:S(2)}, u32[]{:S(2)}) collective-permute-start(bf16[1536,128]{1,0:T(8,128)(2,1)S(1)} %slice.150), channel_id=1, source_target_pairs={{1,0},{5,4},{9,8},{13,12},{17,16},{21,20},{25,24},{29,28}} | collective-permute-start | bytes 1179656 | tf_op jit(solution)/shard_map/ppermute | solution.py:345
  118.1 16.5 %collective-permute-start.2 = (s32[4,257]{1,0:T(4,128)S(1)}, s32[4,257]{1,0:T(4,128)S(1)}, u32[]{:S(2)}, u32[]{:S(2)}) collective-permute-start(s32[4,257]{1,0:T(4,128)S(1)} %get-tuple-element.24), channel_id=1, source_target_pairs={{0,8},{8,0},{4,12},{12,4},{16,24},{24,16},{20,28},{28,20},{1,9},{9... | collective-permute-start | bytes 12344 | tf_op jit(solution)/shard_map/ppermute | solution.py:391
  119.3 16.9 %collective-permute-start.32 = (bf16[1,1808,128]{2,1,0:T(8,128)(2,1)S(1)}, bf16[1,1808,128]{2,1,0:T(8,128)(2,1)S(1)}, u32[]{:S(2)}, u32[]{:S(2)}) collective-permute-start(bf16[1,1808,128]{2,1,0:T(8,128)(2,1)S(1)} %collective-permute-done.31.right0), channel_id=1, source_target_pairs={{1,2},{2,3},{5,6},{6,7},{9,10},{10,11},{13,14},{14,15},{17,18},{18... | collective-permute-start | bytes 1388552 | tf_op jit(solution)/shard_map/ppermute | solution.py:345
  120.0 30.1 %collective-permute-start.25 = (bf16[1,1808,128]{2,1,0:T(8,128)(2,1)S(1)}, bf16[1,1808,128]{2,1,0:T(8,128)(2,1)S(1)}, u32[]{:S(2)}, u32[]{:S(2)}) collective-permute-start(bf16[1,1808,128]{2,1,0:T(8,128)(2,1)S(1)} %pad_maximum_fusion.2), channel_id=1, source_target_pairs={{2,3},{6,7},{10,11},{14,15},{18,19},{22,23},{26,27},{30,31}} | collective-permute-start | bytes 1388552 | tf_op jit(solution)/shard_map/ppermute | solution.py:345
  121.6 28.5 %collective-permute-start.22 = (bf16[1536,128]{1,0:T(8,128)(2,1)S(1)}, bf16[1536,128]{1,0:T(8,128)(2,1)S(1)}, u32[]{:S(2)}, u32[]{:S(2)}) collective-permute-start(bf16[1536,128]{1,0:T(8,128)(2,1)S(1)} %slice.154), channel_id=1, source_target_pairs={{1,0},{5,4},{9,8},{13,12},{17,16},{21,20},{25,24},{29,28}} | collective-permute-start | bytes 1179656 | tf_op jit(solution)/shard_map/ppermute | solution.py:345
  132.8 13.6 %collective-permute-start.18 = (bf16[4,256,256]{2,1,0:T(8,128)(2,1)S(1)}, bf16[4,256,256]{2,1,0:T(8,128)(2,1)S(1)}, u32[]{:S(2)}, u32[]{:S(2)}) collective-permute-start(bf16[4,256,256]{2,1,0:T(8,128)(2,1)S(1)} %get-tuple-element.32.own_ref), channel_id=1, source_target_pairs={{0,8},{8,0},{4,12},{12,4},{16,24},{24,16},{20,28},{28,20},{1,9},{9... | collective-permute-start | bytes 1572872 | tf_op jit(solution)/shard_map/ppermute | solution.py:411
  134.6 23.1 %collective-permute-start.28 = (bf16[1808,128]{1,0:T(8,128)(2,1)S(1)}, bf16[1808,128]{1,0:T(8,128)(2,1)}, u32[]{:S(2)}, u32[]{:S(2)}) collective-permute-start(bf16[1808,128]{1,0:T(8,128)(2,1)S(1)} %fusion.3), channel_id=1, source_target_pairs={{1,0},{2,1},{3,2},{5,4},{6,5},{7,6},{9,8},{10,9},{11,10},{13,12},{... | collective-permute-start | bytes 1388552 | tf_op jit(solution)/shard_map/ppermute | solution.py:345
  136.1 34.4 %collective-permute-start.30 = (bf16[1536,128]{1,0:T(8,128)(2,1)}, bf16[1536,128]{1,0:T(8,128)(2,1)}, u32[]{:S(2)}, u32[]{:S(2)}) collective-permute-start(bf16[1536,128]{1,0:T(8,128)(2,1)} %slice.135), channel_id=1, source_target_pairs={{3,0},{7,4},{11,8},{15,12},{19,16},{23,20},{27,24},{31,28}} | collective-permute-start | bytes 1179656 | tf_op jit(solution)/shard_map/ppermute | solution.py:345
  146.4 12.8 %collective-permute-start.1 = (s32[4,257]{1,0:T(4,128)S(1)}, s32[4,257]{1,0:T(4,128)S(1)}, u32[]{:S(2)}, u32[]{:S(2)}) collective-permute-start(s32[4,257]{1,0:T(4,128)S(1)} %get-tuple-element.23), channel_id=1, source_target_pairs={{0,16},{16,0},{4,20},{20,4},{8,24},{24,8},{12,28},{28,12},{1,17},{... | collective-permute-start | bytes 12344 | tf_op jit(solution)/shard_map/ppermute | solution.py:391
  154.0 13.1 %collective-permute-start.26 = (bf16[4,256,256]{2,1,0:T(8,128)(2,1)S(1)}, bf16[4,256,256]{2,1,0:T(8,128)(2,1)S(1)}, u32[]{:S(2)}, u32[]{:S(2)}) collective-permute-start(bf16[4,256,256]{2,1,0:T(8,128)(2,1)S(1)} %get-tuple-element.37.own_ref), channel_id=1, source_target_pairs={{0,16},{16,0},{4,20},{20,4},{8,24},{24,8},{12,28},{28,12},{1,17},{... | collective-permute-start | bytes 1572872 | tf_op jit(solution)/shard_map/ppermute | solution.py:411
  156.3 14.3 %collective-permute-start.33 = (bf16[1,1808,128]{2,1,0:T(8,128)(2,1)}, bf16[1,1808,128]{2,1,0:T(8,128)(2,1)}, u32[]{:S(2)}, u32[]{:S(2)}) collective-permute-start(bf16[1,1808,128]{2,1,0:T(8,128)(2,1)} %pad_maximum_fusion.3), channel_id=1, source_target_pairs={{2,3},{6,7},{10,11},{14,15},{18,19},{22,23},{26,27},{30,31}} | collective-permute-start | bytes 1388552 | tf_op jit(solution)/shard_map/ppermute | solution.py:345
  157.7 12.9 %collective-permute-start.29 = (bf16[1808,128]{1,0:T(8,128)(2,1)}, bf16[1808,128]{1,0:T(8,128)(2,1)}, u32[]{:S(2)}, u32[]{:S(2)}) collective-permute-start(bf16[1808,128]{1,0:T(8,128)(2,1)} %collective-permute-done.28.left1), channel_id=1, source_target_pairs={{1,0},{2,1},{5,4},{6,5},{9,8},{10,9},{13,12},{14,13},{17,16},{18,1... | collective-permute-start | bytes 1388552 | tf_op jit(solution)/shard_map/ppermute | solution.py:345
  (33 other events, 429.0 us)
